TPU v7x, 32 devices: a whole 2x2x4 slice. The times are simulated.
32 devices in a mesh: span: 4 (over y, x), plane: 8 (over z, core).
Axes of the slice: x: 2, y: 2, z: 4, core: 2. Of those that a mesh axis runs over, the one named last changes fastest.
Arguments:
- state: float32 [512, 40, 640], P('span', 'plane'), may hold values from -8 to 8, as said below
- wall_tag: int32 [128], replicated, may hold values 0 or 1
Outputs:
- new_state: float32 [512, 40, 640], P('span', 'plane')
Inputs may be any that keep to these rules, and one draw needn't show every extreme that they name: `state`: spectral coefficients of the conserved variable.
All inputs are finite; a program needn't handle non-finite values.
Results may differ from a plain program's by a relative error of at most 0.0001.
Values sent between devices are 32-bit elements; how exact they have to be, the bound alone decides.
A program may use at most 64 MiB of HBM per device.

v0:
```python
import functools
import math

import jax
import jax.numpy as jnp
import numpy as np
from jax import lax
from jax.experimental import pallas as pl
from jax.experimental.pallas import tpu as pltpu
from jax.sharding import PartitionSpec as P

KMODES = 256
PLANES = 768
STEP = 0.03
VISCOUS = 0.05
STIFF = 4.0
PAD = 16

f32 = jnp.float32
bf16 = jnp.bfloat16
NT = (((1,), (1,)), ((), ()))
NN = (((1,), (0,)), ((), ()))
TN = (((0,), (0,)), ((), ()))
VMEM_LIMIT = 56 * 1024 * 1024


def gll_tables():
    x = np.array([-1.0, -math.sqrt(3.0 / 7.0), 0.0, math.sqrt(3.0 / 7.0), 1.0])
    w = np.array([0.1, 49.0 / 90.0, 32.0 / 45.0, 49.0 / 90.0, 0.1])
    q = x * x
    leg = (35.0 * q * q - 30.0 * q + 3.0) / 8.0
    eye = np.eye(5)
    d = np.where(eye > 0, 0.0, leg[:, None] / leg[None, :] / (x[:, None] - x[None, :] + eye))
    d[0, 0], d[4, 4] = -5.0, 5.0
    return d, w, d.T @ (w[:, None] * d)


DIFF, WEIGHT, KMAT = gll_tables()


def halves(table):
    high = table.astype(np.float32).astype(bf16)
    low = (table.astype(np.float32) - high.astype(np.float32)).astype(bf16)
    return high, low


def basis_tables():
    k, p = np.arange(KMODES), np.arange(PLANES)
    angle = 2.0 * math.pi * (p[:, None] * k[None, :] % PLANES) / PLANES
    cos, sin = np.cos(angle), np.sin(angle)
    inverse = np.stack([cos, sin], 2).reshape(PLANES, 2 * KMODES).T / math.sqrt(KMODES)
    factor = np.where(k == 0, 1.0, 2.0) * (math.sqrt(KMODES) / PLANES) * STEP
    ratio = k / KMODES
    inner = np.stack([cos * factor, sin * factor], 2).reshape(PLANES, 2 * KMODES)
    span = np.stack([-ratio * sin * factor, ratio * cos * factor], 2).reshape(PLANES, 2 * KMODES)
    return inverse, inner, span


def split2(x):
    high = x.astype(bf16)
    return high, (x - high.astype(f32)).astype(bf16)


def split3(x):
    high = x.astype(bf16)
    rest = x - high.astype(f32)
    mid = rest.astype(bf16)
    return high, mid, (rest - mid.astype(f32)).astype(bf16)


def dot(a, b, dims=NN):
    return lax.dot_general(a, b, dims, preferred_element_type=f32)


def along(mat, a, flip):
    s1, d1, s2, d2, m = a[0] + a[4], a[0] - a[4], a[1] + a[3], a[1] - a[3], a[2]
    out = [None] * 5
    for r in (0, 1):
        e = [0.5 * (mat[r][b] + mat[r][4 - b]) for b in (0, 1)]
        o = [0.5 * (mat[r][b] - mat[r][4 - b]) for b in (0, 1)]
        even = float(e[0]) * s1 + float(e[1]) * s2 + float(mat[r][2]) * m
        odd = float(o[0]) * d1 + float(o[1]) * d2
        out[r] = even + odd
        out[4 - r] = even - odd if flip > 0 else odd - even
    if flip > 0:
        out[2] = float(mat[2][0]) * s1 + float(mat[2][1]) * s2 + float(mat[2][2]) * m
    else:
        out[2] = float(mat[2][0]) * d1 + float(mat[2][1]) * d2
    return out


def two_point10(a, b, qa, qb):
    speed = jnp.maximum(jnp.abs(a), jnp.abs(b))
    return (qa + a * b + qb) * (10.0 / 6.0) - 5.0 * speed * (b - a)


def roll(x, by):
    return pltpu.roll(x, by % x.shape[0], 0)


def pack(x_ref, perm_ref, d_ref, span, elems):
    modes, rows, cols = x_ref.shape
    block = 5 * elems
    x = jnp.concatenate([x_ref[:, j, :] for j in range(rows)], axis=0)
    parts = split3(x)
    for s in range(span):
        lo = block * s // 128 * 128
        hi = -(-block * (s + 1) // 128) * 128
        perm = perm_ref[s, :, : hi - lo]
        got = sum(dot(perm, part[:, lo:hi], NT) for part in parts)
        for j in range(rows):
            d_ref[s, block * j : block * (j + 1), :] = got[:, modes * j : modes * (j + 1)]
    for s in range(span):
        left, right = (s - 1) % span, (s + 1) % span
        for j in range(rows):
            at = block * rows + 2 * j
            last = block * j + block - 1
            d_ref[s, at : at + 1, :] = d_ref[left, last : last + 1, :]
            d_ref[s, at + 1 : at + 2, :] = d_ref[right, block * j : block * j + 1, :]
        for at in range(block * rows + 2 * rows, block * rows + PAD):
            d_ref[s, at : at + 1, :] = jnp.zeros((1, modes), f32)


def perm_tables(span, elems):
    block = 5 * elems
    width = max(-(-block * (s + 1) // 128) * 128 - block * s // 128 * 128 for s in range(span))
    perm = np.zeros((span, block, width), np.float32)
    for s in range(span):
        lo = block * s // 128 * 128
        for i in range(5):
            for e in range(elems):
                perm[s, i * elems + e, block * s + 5 * e + i - lo] = 1.0
    return perm.astype(bf16)


def physical(recv_ref, below_ref, above_ref, tag_ref, inv_ref, fld_ref, elems, first, last):
    span, sr, modes = recv_ref.shape
    block = 5 * elems
    x = jnp.concatenate(
        [
            jnp.concatenate([ref[s] for s in range(span)], axis=1)
            for ref in (recv_ref, below_ref, above_ref)
        ],
        axis=0,
    )
    high, low = split2(x)
    step = 256
    for n in range(PLANES // step):
        at = slice(n * step, (n + 1) * step)
        bh, bl = inv_ref[0, :, at], inv_ref[1, :, at]
        fld_ref[:, at] = dot(high, bh) + dot(high, bl) + dot(low, bh)
    own0 = fld_ref[0:block, :]
    mirror = jnp.where(tag_ref[...] == 1, -own0, own0)
    fld_ref[sr : sr + block, :] = jnp.where(first, mirror, fld_ref[sr : sr + block, :])
    own4 = fld_ref[4 * block : 5 * block, :]
    fld_ref[sr + block : sr + 2 * block, :] = jnp.where(
        last, own4, fld_ref[sr + block : sr + 2 * block, :]
    )


def pointwise(fld_ref, r_ref, h_ref, elems):
    block = 5 * elems
    sr = 5 * block + PAD
    lane = 128
    third = DIFF * (-1.0 / 3.0)

    def body(n, _):
        at = pl.ds(pl.multiple_of(n * lane, lane), lane)
        row = lax.broadcasted_iota(jnp.int32, (elems, lane), 0)

        def load(k):
            return fld_ref[k : k + elems, at]

        u = [[load(block * j + elems * i) for i in range(5)] for j in range(5)]
        q = [[v * v for v in r] for r in u]
        rhs = [[None] * 5 for _ in range(5)]
        for j in range(5):
            du = along(third, u[j], -1)
            dq = along(third, q[j], -1)
            for i in range(5):
                rhs[j][i] = dq[i] + u[j][i] * du[i]
            hl = fld_ref[5 * block + 2 * j : 5 * block + 2 * j + 1, at]
            hr = fld_ref[5 * block + 2 * j + 1 : 5 * block + 2 * j + 2, at]
            left = jnp.where(row == 0, hl, roll(u[j][4], 1))
            right = jnp.where(row == elems - 1, hr, roll(u[j][0], -1))
            rhs[j][0] += two_point10(left, u[j][0], left * left, q[j][0]) - 5.0 * q[j][0]
            rhs[j][4] -= two_point10(u[j][4], right, q[j][4], right * right) - 5.0 * q[j][4]
        for i in range(5):
            ui, qi = [u[j][i] for j in range(5)], [q[j][i] for j in range(5)]
            du = along(third, ui, -1)
            dq = along(third, qi, -1)
            for j in range(5):
                rhs[j][i] += dq[j] + ui[j] * du[j]
            lower = load(sr + elems * i)
            upper = load(sr + block + elems * i)
            rhs[0][i] += two_point10(lower, ui[0], lower * lower, qi[0]) - 5.0 * qi[0]
            rhs[4][i] -= two_point10(ui[4], upper, qi[4], upper * upper) - 5.0 * qi[4]
        for ref, val, scale in ((r_ref, rhs, None), (h_ref, q, 0.5)):
            for j in range(5):
                a = val[j] if scale is None else [scale * v for v in val[j]]
                ref[4 * elems * j : 4 * elems * j + elems, at] = a[0] + jnp.where(
                    row == 0, 0.0, roll(a[4], 1)
                )
                for i in (1, 2, 3):
                    k = elems * (4 * j + i)
                    ref[k : k + elems, at] = a[i]
                ref[20 * elems + j : 20 * elems + j + 1, at] = a[4][elems - 1 : elems, :]
            ref[20 * elems + 5 : 20 * elems + PAD, at] = jnp.zeros((PAD - 5, lane), f32)
        return 0

    lax.fori_loop(0, PLANES // lane, body, 0)


def spectral(r_ref, h_ref, fwd_ref, t_ref):
    span, _, modes = t_ref.shape
    rh, rl = split2(r_ref[...])
    hh, hl = split2(h_ref[...])
    step = max(modes, 256)
    for n in range(span * modes // step):
        at = slice(n * step, (n + 1) * step)
        a, b = fwd_ref[0, :, at], fwd_ref[1, :, at]
        c, d = fwd_ref[2, :, at], fwd_ref[3, :, at]
        t = dot(rh, a) + dot(rl, a) + dot(rh, b) + dot(hh, c) + dot(hl, c) + dot(hh, d)
        for k in range(step // modes):
            t_ref[n * (step // modes) + k] = t[:, modes * k : modes * (k + 1)]


def column_load(d_ref, t_ref, c_ref, elems):
    span, _, modes = d_ref.shape
    block = 5 * elems
    total = span * elems
    row = lax.broadcasted_iota(jnp.int32, (elems, modes), 0)
    for j in range(5):
        for s in range(span):
            left = (s - 1) % span
            for i in range(4):
                k = block * j + elems * i
                val = d_ref[s, k : k + elems, :] + t_ref[s, elems * (4 * j + i) : elems * (4 * j + i + 1), :]
                if i == 0:
                    k4 = block * j + 4 * elems
                    extra = 20 * elems + j
                    edge = d_ref[left, k4 + elems - 1 : k4 + elems, :] + t_ref[left, extra : extra + 1, :]
                    val += jnp.where(row == 0, edge, roll(d_ref[s, k4 : k4 + elems, :], 1))
                c_ref[j, i, elems * s : elems * (s + 1), :] = val * float(WEIGHT[j] * WEIGHT[i])


def apply_local(v_ref, out_ref, shift):
    col = [2.0 * WEIGHT[0], WEIGHT[1], WEIGHT[2], WEIGHT[3]]
    for j in range(5):
        a = [v_ref[j, i] for i in range(4)]
        a.append(roll(a[0], -1))
        kx = along(KMAT * (VISCOUS * WEIGHT[j]), a, 1)
        kx[0] = kx[0] + roll(kx[4], 1)
        for i in range(4):
            out_ref[j, i] = kx[i]
    total = 0.0
    for i in range(4):
        a = [v_ref[j, i] for j in range(5)]
        ky = along(KMAT * (VISCOUS * col[i]), a, 1)
        for j in range(5):
            val = out_ref[j, i] + ky[j] + (shift * float(WEIGHT[j] * col[i])) * a[j]
            out_ref[j, i] = val
            total = total + jnp.sum(val * a[j], axis=0, keepdims=True)
    return total


def square_sum(v_ref, first, last):
    total = 0.0
    for j in range(5):
        part = sum(jnp.sum(v_ref[j, i] * v_ref[j, i], axis=0, keepdims=True) for i in range(4))
        if j == 0:
            part = part * jnp.where(first, 1.0, 0.5)
        if j == 4:
            part = part * jnp.where(last, 1.0, 0.5)
        total = total + part
    return total


def solve3(nu, theta):
    a = [[nu[r + c + 1] + theta * nu[r + c] for c in range(3)] for r in range(3)]
    l10, l20 = a[1][0] / a[0][0], a[2][0] / a[0][0]
    d1 = a[1][1] - l10 * a[1][0]
    e = a[2][1] - l20 * a[1][0]
    l21 = e / d1
    d2 = a[2][2] - l20 * a[2][0] - l21 * e
    z0 = nu[0]
    z1 = nu[1] - l10 * z0
    z2 = nu[2] - l20 * z0 - l21 * z1
    y2 = z2 / d2
    y1 = z1 / d1 - l21 * y2
    return z0 / a[0][0] - l10 * y1 - l20 * y2, y1, y2


def unpack(v0_ref, v1_ref, v2_ref, y_ref, exp_ref, out_ref):
    elems, modes = v0_ref.shape[2:]
    y = [y_ref[k : k + 1, :] for k in range(3)]
    for j in range(5):
        x = jnp.concatenate(
            [y[0] * v0_ref[j, i] + y[1] * v1_ref[j, i] + y[2] * v2_ref[j, i] for i in range(4)], axis=0
        )
        out_ref[:, j, :] = sum(dot(part, exp_ref[...], TN) for part in split2(x))


def expand_table(total):
    out = np.zeros((4 * total, 5 * total), np.float32)
    for e in range(total):
        for i in range(5):
            out[(i % 4) * total + (e + i // 4) % total, 5 * e + i] = 1.0
    return out.astype(bf16)


def call(body, outs, scratch=(), **kw):
    return pl.pallas_call(
        body,
        out_shape=outs,
        scratch_shapes=list(scratch),
        compiler_params=pltpu.CompilerParams(vmem_limit_bytes=VMEM_LIMIT),
        **kw,
    )


def shape(*dims):
    return jax.ShapeDtypeStruct(dims, f32)


def on_device(state, wall_tag):
    modes, rows, cols = state.shape
    assert rows == 5
    span, planes = lax.axis_size("span"), lax.axis_size("plane")
    total = cols // 5
    elems = total // span
    block = 5 * elems
    sr, tr = 5 * block + PAD, 20 * elems + PAD
    my_span, my_plane = lax.axis_index("span"), lax.axis_index("plane")
    first, last = my_plane == 0, my_plane == planes - 1
    up = [(i, i + 1) for i in range(planes - 1)]
    down = [(i + 1, i) for i in range(planes - 1)]

    inverse, inner, outer = basis_tables()
    inv = jnp.asarray(np.stack(halves(inverse)))
    fwd = jnp.asarray(np.stack(halves(inner) + halves(outer)))
    perm = jnp.asarray(perm_tables(span, elems))
    expand = jnp.asarray(expand_table(total))
    ids = my_span * modes + jnp.arange(modes, dtype=jnp.int32)
    wave = (ids // 2).astype(f32) / KMODES
    shift = (1.0 + STIFF * wave * wave)[None, :]
    theta = 0.6 + 0.254 * (shift - 1.0)
    tags = jnp.tile(lax.dynamic_slice_in_dim(wall_tag, my_span * elems, elems, 0), 5)[:, None]
    edge = jnp.stack([first, last]).astype(jnp.int32)
    smem = pl.BlockSpec(memory_space=pltpu.SMEM)
    vmem = pl.BlockSpec(memory_space=pltpu.VMEM)

    own = call(lambda x, p, d: pack(x, p, d, span, elems), shape(span, sr, modes))(state, perm)
    recv = lax.all_to_all(own, "span", 0, 0, tiled=True)
    below = lax.ppermute(recv[:, 4 * block : 5 * block], "plane", up)
    above = lax.ppermute(recv[:, :block], "plane", down)

    def middle(edge_ref, x, lo, hi, tag, inv_ref, fwd_ref, t_ref, fld, r, h):
        physical(x, lo, hi, tag, inv_ref, fld, elems, edge_ref[0] == 1, edge_ref[1] == 1)
        pointwise(fld, r, h, elems)
        spectral(r, h, fwd_ref, t_ref)

    sent = call(
        middle,
        shape(span, tr, modes),
        [
            pltpu.VMEM((sr + 2 * block, PLANES), f32),
            pltpu.VMEM((tr, PLANES), f32),
            pltpu.VMEM((tr, PLANES), f32),
        ],
        in_specs=[smem] + [vmem] * 6,
        out_specs=vmem,
    )(edge, recv, below, above, tags, inv, fwd)
    got = lax.all_to_all(sent, "span", 0, 0, tiled=True)
    joined = shape(5, 4, total, modes)
    part = call(lambda d, t, c: column_load(d, t, c, elems), joined)(own, got)

    def join(c):
        return lax.ppermute(c[4], "plane", up), lax.ppermute(c[0], "plane", down)

    def row_join(c, lo, hi, prev, theta_ref, v):
        for j in range(5):
            for i in range(4):
                val = c[j, i]
                if j == 0:
                    val = val + lo[i]
                if j == 4:
                    val = val + hi[i]
                if prev is not None:
                    val = val - theta_ref[...] * prev[j, i]
                v[j, i] = val

    row = shape(1, modes)

    def step0(edge_ref, c, lo, hi, th, sh, v, out, sq, dt):
        row_join(c, lo, hi, None, None, v)
        sq[...] = square_sum(v, edge_ref[0] == 1, edge_ref[1] == 1)
        dt[...] = apply_local(v, out, sh[...])

    def step1(edge_ref, c, lo, hi, prev, th, sh, v, out, sq, dt):
        row_join(c, lo, hi, prev, th, v)
        sq[...] = square_sum(v, edge_ref[0] == 1, edge_ref[1] == 1)
        dt[...] = apply_local(v, out, sh[...])

    def finish(edge_ref, c, lo, hi, prev, th, sh, v, sq, dt, out):
        step1(edge_ref, c, lo, hi, prev, th, sh, v, out, sq, dt)

    v0, c1, s0, t0 = call(step0, (joined, joined, row, row), in_specs=[smem] + [vmem] * 5)(
        edge, part, *join(part), theta, shift
    )
    v1, c2, s1, t1 = call(step1, (joined, joined, row, row), in_specs=[smem] + [vmem] * 6)(
        edge, c1, *join(c1), v0, theta, shift
    )
    v2, s2, t2 = call(
        finish,
        (joined, row, row),
        [pltpu.VMEM(joined.shape, f32)],
        in_specs=[smem] + [vmem] * 6,
    )(edge, c2, *join(c2), v1, theta, shift)
    sums = lax.psum(jnp.concatenate([s0, t0, s1, t1, s2, t2], axis=0), "plane")
    n0, h0, n2, h2, n4, h4 = [sums[k : k + 1] for k in range(6)]
    nu = [n0, h0 - theta * n0, n2, h2 - theta * n2, n4, h4 - theta * n4]
    y = jnp.concatenate(solve3(nu, theta), axis=0)
    return call(unpack, shape(modes, rows, cols))(v0, v1, v2, y, expand)


def solution(mesh):
    spec = P("span", "plane", None)
    return jax.shard_map(
        on_device, mesh=mesh, in_specs=(spec, P()), out_specs=spec, check_vma=False
    )
```

profile of v0, /device:TPU:0, one launch (start us, length us, event | category | flops | bytes accessed | tf_op | source)
XLA Modules:
  0.0 153.3 jit_solution(3691149189794095262)
XLA Ops:
  0.0 4.0 %copy.9.x = f32[128,5,640]{2,1,0:T(8,128)} copy(f32[128,5,640]{2,0,1:T(8,128)} %param.6) | data formatting | bytes 3276800 | tf_op args[0]
  4.0 4.7 %shard_map.64.d = f32[4,816,128]{2,1,0:T(8,128)} custom-call(f32[128,5,640]{2,1,0:T(8,128)} %copy.9.x, bf16[4,160,256]{2,1,0:T(8,128)(2,1)} %constant.54.clone.p), custom_call_target="tpu_custom_call" | custom-call | tf_op jit(solution)/shard_map/pallas_call | solution.py:353
  8.7 26.2 %all_to_all.10.x = f32[4,816,128]{2,1,0:T(8,128)S(1)} all-to-all(f32[4,816,128]{2,1,0:T(8,128)} %shard_map.64.d), channel_id=1, replica_groups=mesh['span'=4,'plane'=8] {'span'}, dimensions={0} | all-to-all | bytes 3342336 | tf_op jit(solution)/shard_map/all_to_all | solution.py:354
  34.9 1.3 collective-permute-start.1
  36.2 3.1 %collective-permute-start = (f32[4,160,128]{2,1,0:T(8,128)S(1)}, f32[4,160,128]{2,1,0:T(8,128)S(1)}, u32[]{:S(2)}, u32[]{:S(2)}) collective-permute-start(f32[4,160,128]{2,1,0:T(8,128)S(1)} %get-tuple-element.36), channel_id=1, source_target_pairs={{0,1},{1,2},{2,3},{3,4},{4,5},{5,6},{6,7},{8,9},{9,10},{10,11},{11... | collective-permute-start | bytes 983048 | tf_op jit(solution)/shard_map/ppermute | solution.py:355
  39.3 0.1 dynamic_slice.3
  39.4 0.7 broadcast_in_dim_tile.4.tag
  40.1 0.6 add_convert_fusion.edge_ref
  40.8 0.0 collective-permute-done.1.hi
  40.8 0.0 collective-permute-done.lo
  40.8 0.0 copy-done
  40.8 0.7 copy-done.1
  41.5 0.7 copy-done.2
  42.2 14.0 %shard_map.65 = f32[4,656,128]{2,1,0:T(8,128)} custom-call(s32[2]{0:T(128)} %add_convert_fusion.edge_ref, f32[4,816,128]{2,1,0:T(8,128)} %copy-done, f32[4,160,128]{2,1,0:T(8,128)} %copy-done.2, f32[4,160,128]{2,1,0:T(8,128)} %copy-done.1, s32[160,1]{1,0:T(8,128)} %broadcast_in_dim_tile.4.tag, bf16[2,512,768]{2,1,0:T(8,128)(2,1)} %constant.52.clone.inv_ref, ...), custom_call_target="tpu_custom_call" | custom-call | tf_op jit(solution)/shard_map/pallas_call | solution.py:363
  56.2 21.1 %all_to_all.11.t = f32[4,656,128]{2,1,0:T(8,128)} all-to-all(f32[4,656,128]{2,1,0:T(8,128)} %shard_map.65), channel_id=1, replica_groups=mesh['span'=4,'plane'=8] {'span'}, dimensions={0} | all-to-all | bytes 2686976 | tf_op jit(solution)/shard_map/all_to_all | solution.py:374
  77.3 3.1 %shard_map.66.c = f32[5,4,128,128]{3,2,1,0:T(8,128)} custom-call(f32[4,816,128]{2,1,0:T(8,128)} %shard_map.64.d, f32[4,656,128]{2,1,0:T(8,128)} %all_to_all.11.t), custom_call_target="tpu_custom_call" | custom-call | tf_op jit(solution)/shard_map/pallas_call | solution.py:376
  80.4 1.1 slice_bitcast_fusion
  81.5 1.3 collective-permute-start.3
  82.8 4.6 %collective-permute-start.2 = (f32[4,128,128]{2,1,0:T(8,128)S(1)}, f32[4,128,128]{2,1,0:T(8,128)S(1)}, u32[]{:S(2)}, u32[]{:S(2)}) collective-permute-start(f32[4,128,128]{2,1,0:T(8,128)S(1)} %get-tuple-element.42), channel_id=1, source_target_pairs={{0,1},{1,2},{2,3},{3,4},{4,5},{5,6},{6,7},{8,9},{9,10},{10,11},{11... | collective-permute-start | bytes 786440 | tf_op jit(solution)/shard_map/ppermute | solution.py:379
  87.4 0.6 multiply_add_fusion.1
  88.0 0.0 collective-permute-done.3.hi
  88.0 0.5 collective-permute-done.2.lo
  88.5 0.2 copy-done.7
  88.7 0.5 copy-done.8
  89.2 3.6 %shard_map.67 = (f32[5,4,128,128]{3,2,1,0:T(8,128)}, f32[5,4,128,128]{3,2,1,0:T(8,128)}, f32[1,128]{1,0:T(1,128)}, f32[1,128]{1,0:T(1,128)}) custom-call(s32[2]{0:T(128)} %add_convert_fusion.edge_ref, f32[5,4,128,128]{3,2,1,0:T(8,128)} %shard_map.66.c, f32[4,128,128]{2,1,0:T(8,128)} %copy-done.8, f32[4,128,128]{2,1,0:T(8,128)} %copy-done.7, ...), custom_call_target="tpu_custom_call" | custom-call | tf_op jit(solution)/shard_map/pallas_call | solution.py:408
  92.9 1.1 slice_bitcast_fusion.4
  94.0 1.3 collective-permute-start.5
  95.3 8.9 %collective-permute-start.4 = (f32[4,128,128]{2,1,0:T(8,128)S(1)}, f32[4,128,128]{2,1,0:T(8,128)S(1)}, u32[]{:S(2)}, u32[]{:S(2)}) collective-permute-start(f32[4,128,128]{2,1,0:T(8,128)S(1)} %get-tuple-element.40), channel_id=1, source_target_pairs={{0,1},{1,2},{2,3},{3,4},{4,5},{5,6},{6,7},{8,9},{9,10},{10,11},{11... | collective-permute-start | bytes 786440 | tf_op jit(solution)/shard_map/ppermute | solution.py:379
  104.1 0.0 collective-permute-done.5.hi
  104.2 0.0 copy-start.4
  104.2 0.9 collective-permute-done.4.lo
  105.1 0.0 copy-done.4
  105.1 0.7 copy-done.6
  105.8 4.1 %shard_map.68 = (f32[5,4,128,128]{3,2,1,0:T(8,128)}, f32[5,4,128,128]{3,2,1,0:T(8,128)}, f32[1,128]{1,0:T(1,128)}, f32[1,128]{1,0:T(1,128)}) custom-call(s32[2]{0:T(128)} %add_convert_fusion.edge_ref, f32[5,4,128,128]{3,2,1,0:T(8,128)} %get-tuple-element.17.c, f32[4,128,128]{2,1,0:T(8,128)} %copy-done.6, f32[4,128,128]{2,1,0:T(8,128)} %copy-done.4, ...), custom_call_target="tpu_custom_call" | custom-call | tf_op jit(solution)/shard_map/pallas_call | solution.py:411
  109.9 1.1 slice_bitcast_fusion.2
  111.0 1.3 collective-permute-start.7
  112.3 7.2 %collective-permute-start.6 = (f32[4,128,128]{2,1,0:T(8,128)S(1)}, f32[4,128,128]{2,1,0:T(8,128)S(1)}, u32[]{:S(2)}, u32[]{:S(2)}) collective-permute-start(f32[4,128,128]{2,1,0:T(8,128)S(1)} %get-tuple-element.38), channel_id=1, source_target_pairs={{0,1},{1,2},{2,3},{3,4},{4,5},{5,6},{6,7},{8,9},{9,10},{10,11},{11... | collective-permute-start | bytes 786440 | tf_op jit(solution)/shard_map/ppermute | solution.py:379
  119.5 0.0 collective-permute-done.7.hi
  119.5 1.1 collective-permute-done.6.lo
  120.6 0.0 copy-done.3
  120.6 0.7 copy-done.5
  121.3 3.7 %shard_map.69 = (f32[5,4,128,128]{3,2,1,0:T(8,128)}, f32[1,128]{1,0:T(1,128)}, f32[1,128]{1,0:T(1,128)}) custom-call(s32[2]{0:T(128)} %add_convert_fusion.edge_ref, f32[5,4,128,128]{3,2,1,0:T(8,128)} %get-tuple-element.19.c, f32[4,128,128]{2,1,0:T(8,128)} %copy-done.5, f32[4,128,128]{2,1,0:T(8,128)} %copy-done.3, ...), custom_call_target="tpu_custom_call" | custom-call | tf_op jit(solution)/shard_map/pallas_call | solution.py:414
  125.0 0.0 copy-done.9
  125.0 0.7 concatenate.6
  125.7 18.3 %psum.7 = f32[6,128]{1,0:T(8,128)S(1)} all-reduce(f32[6,128]{1,0:T(8,128)S(1)} %concatenate.6), channel_id=1, replica_groups=mesh['span'=4,'plane'=8] {'plane'}, use_global_device_ids=true, to_apply=%region_0.1 | all-reduce | flops 768 | bytes 6144 | tf_op jit(solution)/shard_map/psum | solution.py:420
  144.0 0.6 pad_maximum_fusion.y_ref
  144.6 5.5 %shard_map.70 = f32[128,5,640]{2,1,0:T(8,128)} custom-call(f32[5,4,128,128]{3,2,1,0:T(8,128)} %get-tuple-element.16.prev.v0_ref, f32[5,4,128,128]{3,2,1,0:T(8,128)} %get-tuple-element.18.prev.v1_ref, f32[5,4,128,128]{3,2,1,0:T(8,128)} %get-tuple-element.20.v2_ref, f32[3,128]{1,0:T(4,128)} %pad_maximum_fusion.y_ref, bf16[512,640]{1,0:T(8,128)(2,1)} %constant.55.clone.exp_ref), custom_call_target="tpu_custom_call" | custom-call | tf_op jit(solution)/shard_map/pallas_call | solution.py:424
  150.1 3.2 %copy.11 = f32[128,5,640]{2,0,1:T(8,128)} copy(f32[128,5,640]{2,1,0:T(8,128)} %shard_map.70) | data formatting | bytes 3276800 | tf_op jit(solution)/shard_map/pallas_call | solution.py:424
  (22 shorter events, 0.2 us)
Async XLA Ops:
  8.7 30.6 %copy-start.13 = (s32[128]{0:T(128)S(1)}, s32[128]{0:T(128)}, u32[]{:S(2)}) copy-start(s32[128]{0:T(128)} %param.7) | copy-start | bytes 1540
  34.9 5.9 %copy-start = (f32[4,816,128]{2,1,0:T(8,128)}, f32[4,816,128]{2,1,0:T(8,128)S(1)}, u32[]{:S(2)}) copy-start(f32[4,816,128]{2,1,0:T(8,128)S(1)} %all_to_all.10.x) | copy-start | bytes 5013508
  34.9 5.8 %collective-permute-start.1 = (f32[4,160,128]{2,1,0:T(8,128)S(1)}, f32[4,160,128]{2,1,0:T(8,128)S(1)}, u32[]{:S(2)}, u32[]{:S(2)}) collective-permute-start(f32[4,160,128]{2,1,0:T(8,128)S(1)} %get-tuple-element.35), channel_id=1, source_target_pairs={{1,0},{2,1},{3,2},{4,3},{5,4},{6,5},{7,6},{9,8},{10,9},{11,10},{12... | collective-permute-start | bytes 983048 | tf_op jit(solution)/shard_map/ppermute | solution.py:356
  36.2 4.5 %collective-permute-start = (f32[4,160,128]{2,1,0:T(8,128)S(1)}, f32[4,160,128]{2,1,0:T(8,128)S(1)}, u32[]{:S(2)}, u32[]{:S(2)}) collective-permute-start(f32[4,160,128]{2,1,0:T(8,128)S(1)} %get-tuple-element.36), channel_id=1, source_target_pairs={{0,1},{1,2},{2,3},{3,4},{4,5},{5,6},{6,7},{8,9},{9,10},{10,11},{11... | collective-permute-start | bytes 983048 | tf_op jit(solution)/shard_map/ppermute | solution.py:355
  40.8 0.7 copy-start.1
  41.5 0.7 copy-start.2
  81.5 6.6 %collective-permute-start.3 = (f32[4,128,128]{2,1,0:T(8,128)S(1)}, f32[4,128,128]{2,1,0:T(8,128)S(1)}, u32[]{:S(2)}, u32[]{:S(2)}) collective-permute-start(f32[4,128,128]{2,1,0:T(8,128)S(1)} %get-tuple-element.41), channel_id=1, source_target_pairs={{1,0},{2,1},{3,2},{4,3},{5,4},{6,5},{7,6},{9,8},{10,9},{11,10},{12... | collective-permute-start | bytes 786440 | tf_op jit(solution)/shard_map/ppermute | solution.py:379
  82.8 5.8 %collective-permute-start.2 = (f32[4,128,128]{2,1,0:T(8,128)S(1)}, f32[4,128,128]{2,1,0:T(8,128)S(1)}, u32[]{:S(2)}, u32[]{:S(2)}) collective-permute-start(f32[4,128,128]{2,1,0:T(8,128)S(1)} %get-tuple-element.42), channel_id=1, source_target_pairs={{0,1},{1,2},{2,3},{3,4},{4,5},{5,6},{6,7},{8,9},{9,10},{10,11},{11... | collective-permute-start | bytes 786440 | tf_op jit(solution)/shard_map/ppermute | solution.py:379
  88.0 0.7 copy-start.7
  88.5 0.7 copy-start.8
  94.0 10.2 %collective-permute-start.5 = (f32[4,128,128]{2,1,0:T(8,128)S(1)}, f32[4,128,128]{2,1,0:T(8,128)S(1)}, u32[]{:S(2)}, u32[]{:S(2)}) collective-permute-start(f32[4,128,128]{2,1,0:T(8,128)S(1)} %get-tuple-element.39), channel_id=1, source_target_pairs={{1,0},{2,1},{3,2},{4,3},{5,4},{6,5},{7,6},{9,8},{10,9},{11,10},{12... | collective-permute-start | bytes 786440 | tf_op jit(solution)/shard_map/ppermute | solution.py:379
  95.3 9.8 %collective-permute-start.4 = (f32[4,128,128]{2,1,0:T(8,128)S(1)}, f32[4,128,128]{2,1,0:T(8,128)S(1)}, u32[]{:S(2)}, u32[]{:S(2)}) collective-permute-start(f32[4,128,128]{2,1,0:T(8,128)S(1)} %get-tuple-element.40), channel_id=1, source_target_pairs={{0,1},{1,2},{2,3},{3,4},{4,5},{5,6},{6,7},{8,9},{9,10},{10,11},{11... | collective-permute-start | bytes 786440 | tf_op jit(solution)/shard_map/ppermute | solution.py:379
  104.2 0.9 copy-start.4
  105.1 0.7 copy-start.6
  111.0 8.5 %collective-permute-start.7 = (f32[4,128,128]{2,1,0:T(8,128)S(1)}, f32[4,128,128]{2,1,0:T(8,128)S(1)}, u32[]{:S(2)}, u32[]{:S(2)}) collective-permute-start(f32[4,128,128]{2,1,0:T(8,128)S(1)} %get-tuple-element.37), channel_id=1, source_target_pairs={{1,0},{2,1},{3,2},{4,3},{5,4},{6,5},{7,6},{9,8},{10,9},{11,10},{12... | collective-permute-start | bytes 786440 | tf_op jit(solution)/shard_map/ppermute | solution.py:379
  112.3 8.3 %collective-permute-start.6 = (f32[4,128,128]{2,1,0:T(8,128)S(1)}, f32[4,128,128]{2,1,0:T(8,128)S(1)}, u32[]{:S(2)}, u32[]{:S(2)}) collective-permute-start(f32[4,128,128]{2,1,0:T(8,128)S(1)} %get-tuple-element.38), channel_id=1, source_target_pairs={{0,1},{1,2},{2,3},{3,4},{4,5},{5,6},{6,7},{8,9},{9,10},{10,11},{11... | collective-permute-start | bytes 786440 | tf_op jit(solution)/shard_map/ppermute | solution.py:379
  119.5 1.1 copy-start.3
  120.6 0.7 copy-start.5
  121.3 3.7 %copy-start.9 = (f32[1,128]{1,0:T(1,128)S(1)}, f32[1,128]{1,0:T(1,128)}, u32[]{:S(2)}) copy-start(f32[1,128]{1,0:T(1,128)} %get-tuple-element.21) | copy-start | bytes 1540
  121.3 3.7 %copy-start.10 = (f32[1,128]{1,0:T(1,128)S(1)}, f32[1,128]{1,0:T(1,128)}, u32[]{:S(2)}) copy-start(f32[1,128]{1,0:T(1,128)} %get-tuple-element.22) | copy-start | bytes 1540
  121.3 3.7 %copy-start.11 = (f32[1,128]{1,0:T(1,128)S(1)}, f32[1,128]{1,0:T(1,128)}, u32[]{:S(2)}) copy-start(f32[1,128]{1,0:T(1,128)} %get-tuple-element.23) | copy-start | bytes 1540
  121.3 3.7 %copy-start.12 = (f32[1,128]{1,0:T(1,128)S(1)}, f32[1,128]{1,0:T(1,128)}, u32[]{:S(2)}) copy-start(f32[1,128]{1,0:T(1,128)} %get-tuple-element.24) | copy-start | bytes 1540
where the time goes:
time: 154 us; the launch traced here: 153 us
  blocking collectives  65.5 us (43%)
  Pallas kernels  38.7 us (25%)
  starting transfers between devices  28.9 us (19%)
  local copies, waits for them, and re-layouts  15.5 us (10%)
  waiting for transfers between devices  2.56 us (2%)
  other arithmetic  1.9 us (1%)
    all_to_all x1, blocking collectives, on_device(): recv = lax.all_to_all(own, 'span', 0, 0, tiled=True)  26.2 us
    ppermute x6, starting transfers between devices, join(): return (lax.ppermute(c[4], 'plane', up), lax.ppermute(c[0], 'plane', down))  24.6 us
    all_to_all x1, blocking collectives, on_device(): got = lax.all_to_all(sent, 'span', 0, 0, tiled=True)  21.1 us
    psum x1, blocking collectives, on_device(): sums = lax.psum(jnp.concatenate([s0, t0, s1, t1, s2, t2], axis=0), 'plane')  18.3 us
    pallas_call x1, Pallas kernels, on_device(): call(middle, shape(span, tr, modes), [pltpu.VMEM((sr + 2 * block, PLANES)...  14 us
    unnamed x29, local copies, waits for them, and re-layouts  7.54 us
    pallas_call x1, Pallas kernels, on_device(): return call(unpack, shape(modes, rows, cols))(v0, v1, v2, y, expand)  5.47 us
    pallas_call x1, Pallas kernels, on_device(): call(lambda x, p, d: pack(x, p, d, span, elems), shape(span, sr, modes))  4.74 us
  transfers between devices with their start and end apart: 8, of which 3 were waited for; matrix products, arithmetic and copies ran while one was open for 1% of the time, Pallas kernels for 0%

commit v1 on v0

--- a/solution.py
+++ b/solution.py
@@ -59,13 +59,6 @@
 def split2(x):
     high = x.astype(bf16)
     return high, (x - high.astype(f32)).astype(bf16)
-
-
-def split3(x):
-    high = x.astype(bf16)
-    rest = x - high.astype(f32)
-    mid = rest.astype(bf16)
-    return high, mid, (rest - mid.astype(f32)).astype(bf16)
 
 
 def dot(a, b, dims=NN):
@@ -99,10 +92,9 @@
 
 
 def pack(x_ref, perm_ref, d_ref, span, elems):
-    modes, rows, cols = x_ref.shape
+    rows, modes, cols = x_ref.shape
     block = 5 * elems
-    x = jnp.concatenate([x_ref[:, j, :] for j in range(rows)], axis=0)
-    parts = split3(x)
+    parts = split2(x_ref[...].reshape(rows * modes, cols))
     for s in range(span):
         lo = block * s // 128 * 128
         hi = -(-block * (s + 1) // 128) * 128
@@ -133,29 +125,29 @@
     return perm.astype(bf16)
 
 
-def physical(recv_ref, below_ref, above_ref, tag_ref, inv_ref, fld_ref, elems, first, last):
-    span, sr, modes = recv_ref.shape
-    block = 5 * elems
+def to_planes(parts, inv_ref, fld_ref, lo):
     x = jnp.concatenate(
-        [
-            jnp.concatenate([ref[s] for s in range(span)], axis=1)
-            for ref in (recv_ref, below_ref, above_ref)
-        ],
-        axis=0,
+        [jnp.concatenate([p[s] for s in range(p.shape[0])], axis=1) for p in parts], axis=0
     )
     high, low = split2(x)
-    step = 256
-    for n in range(PLANES // step):
-        at = slice(n * step, (n + 1) * step)
+    for n in range(PLANES // 256):
+        at = slice(n * 256, (n + 1) * 256)
         bh, bl = inv_ref[0, :, at], inv_ref[1, :, at]
-        fld_ref[:, at] = dot(high, bh) + dot(high, bl) + dot(low, bh)
-    own0 = fld_ref[0:block, :]
-    mirror = jnp.where(tag_ref[...] == 1, -own0, own0)
-    fld_ref[sr : sr + block, :] = jnp.where(first, mirror, fld_ref[sr : sr + block, :])
-    own4 = fld_ref[4 * block : 5 * block, :]
-    fld_ref[sr + block : sr + 2 * block, :] = jnp.where(
-        last, own4, fld_ref[sr + block : sr + 2 * block, :]
-    )
+        fld_ref[lo : lo + x.shape[0], at] = dot(high, bh) + dot(high, bl) + dot(low, bh)
+
+
+def outer_rows(fld_ref, tag_ref, elems, first, last):
+    block = 5 * elems
+    sr = 5 * block + PAD
+
+    @pl.when(first)
+    def _():
+        own = fld_ref[0:block, :]
+        fld_ref[sr : sr + block, :] = jnp.where(tag_ref[...] == 1, -own, own)
+
+    @pl.when(last)
+    def _():
+        fld_ref[sr + block : sr + 2 * block, :] = fld_ref[4 * block : 5 * block, :]
 
 
 def pointwise(fld_ref, r_ref, h_ref, elems):
@@ -225,28 +217,38 @@
             t_ref[n * (step // modes) + k] = t[:, modes * k : modes * (k + 1)]
 
 
-def column_load(d_ref, t_ref, c_ref, elems):
-    span, _, modes = d_ref.shape
+def column_load(d_ref, t_ref, c_ref, elems, js):
+    chunks, span, _, modes = t_ref.shape
+    blocks = chunks * span
     block = 5 * elems
-    total = span * elems
     row = lax.broadcasted_iota(jnp.int32, (elems, modes), 0)
-    for j in range(5):
-        for s in range(span):
-            left = (s - 1) % span
+    for j in js:
+        for b in range(blocks):
+            s, k = divmod(b, chunks)
+            left = (b - 1) % blocks
+            sl, kl = divmod(left, chunks)
             for i in range(4):
-                k = block * j + elems * i
-                val = d_ref[s, k : k + elems, :] + t_ref[s, elems * (4 * j + i) : elems * (4 * j + i + 1), :]
+                at = block * j + elems * i
+                tat = elems * (4 * j + i)
+                val = d_ref[b, at : at + elems, :] + t_ref[k, s, tat : tat + elems, :]
                 if i == 0:
-                    k4 = block * j + 4 * elems
+                    at4 = block * j + 4 * elems
                     extra = 20 * elems + j
-                    edge = d_ref[left, k4 + elems - 1 : k4 + elems, :] + t_ref[left, extra : extra + 1, :]
-                    val += jnp.where(row == 0, edge, roll(d_ref[s, k4 : k4 + elems, :], 1))
-                c_ref[j, i, elems * s : elems * (s + 1), :] = val * float(WEIGHT[j] * WEIGHT[i])
-
-
-def apply_local(v_ref, out_ref, shift):
+                    edge = (
+                        d_ref[left, at4 + elems - 1 : at4 + elems, :]
+                        + t_ref[kl, sl, extra : extra + 1, :]
+                    )
+                    val += jnp.where(row == 0, edge, roll(d_ref[b, at4 : at4 + elems, :], 1))
+                c_ref[j, i, elems * b : elems * (b + 1), :] = val * float(WEIGHT[j] * WEIGHT[i])
+
+
+def fold(x):
+    return jnp.sum(x.reshape(x.shape[0] // 8, 8, x.shape[1]), axis=0)
+
+
+def image(v_ref, out_ref, shift, js):
     col = [2.0 * WEIGHT[0], WEIGHT[1], WEIGHT[2], WEIGHT[3]]
-    for j in range(5):
+    for j in js:
         a = [v_ref[j, i] for i in range(4)]
         a.append(roll(a[0], -1))
         kx = along(KMAT * (VISCOUS * WEIGHT[j]), a, 1)
@@ -257,17 +259,27 @@
     for i in range(4):
         a = [v_ref[j, i] for j in range(5)]
         ky = along(KMAT * (VISCOUS * col[i]), a, 1)
-        for j in range(5):
+        for j in js:
             val = out_ref[j, i] + ky[j] + (shift * float(WEIGHT[j] * col[i])) * a[j]
             out_ref[j, i] = val
-            total = total + jnp.sum(val * a[j], axis=0, keepdims=True)
+            total = total + fold(val * a[j])
     return total
 
 
-def square_sum(v_ref, first, last):
+def join_rows(c_ref, lo, hi, prev, theta, v_ref, first, last):
     total = 0.0
-    for j in range(5):
-        part = sum(jnp.sum(v_ref[j, i] * v_ref[j, i], axis=0, keepdims=True) for i in range(4))
+    for j in (0, 4, 1, 2, 3):
+        part = 0.0
+        for i in range(4):
+            val = c_ref[j, i]
+            if j == 0:
+                val = val + lo[i]
+            if j == 4:
+                val = val + hi[i]
+            if prev is not None:
+                val = val - theta * prev[j, i]
+            v_ref[j, i] = val
+            part = part + fold(val * val)
         if j == 0:
             part = part * jnp.where(first, 1.0, 0.5)
         if j == 4:
@@ -291,14 +303,8 @@
     return z0 / a[0][0] - l10 * y1 - l20 * y2, y1, y2
 
 
-def unpack(v0_ref, v1_ref, v2_ref, y_ref, exp_ref, out_ref):
-    elems, modes = v0_ref.shape[2:]
-    y = [y_ref[k : k + 1, :] for k in range(3)]
-    for j in range(5):
-        x = jnp.concatenate(
-            [y[0] * v0_ref[j, i] + y[1] * v1_ref[j, i] + y[2] * v2_ref[j, i] for i in range(4)], axis=0
-        )
-        out_ref[:, j, :] = sum(dot(part, exp_ref[...], TN) for part in split2(x))
+def unpack(x_ref, exp_ref, out_ref):
+    out_ref[0] = sum(dot(part, exp_ref[...], TN) for part in split2(x_ref[0]))
 
 
 def expand_table(total):
@@ -309,14 +315,155 @@
     return out.astype(bf16)
 
 
-def call(body, outs, scratch=(), **kw):
-    return pl.pallas_call(
-        body,
-        out_shape=outs,
-        scratch_shapes=list(scratch),
-        compiler_params=pltpu.CompilerParams(vmem_limit_bytes=VMEM_LIMIT),
-        **kw,
-    )
+def segment(
+    dims, x_ref, perm_ref, tag_ref, shift_ref, theta_ref, inv_hbm, fwd_hbm, out_ref,
+    inv, fwd, d_ref, recv, below, above, fld, r_ref, h_ref, tsend, trecv,
+    c_ref, v0, v1, v2, lo, hi, part, parts,
+    table_sem, s1, r1, s2, r2, s3, r3, s4, r4, s5, r5,
+):
+    span, planes, chunks, elems = dims
+    blocks, bl = span * chunks, 5 * elems
+    sr = 5 * bl + PAD
+    me, mp = lax.axis_index("span"), lax.axis_index("plane")
+    first, last = mp == 0, mp == planes - 1
+    inner, beyond = mp > 0, mp < planes - 1
+    up, down = {"plane": lax.rem(mp + 1, planes)}, {"plane": lax.rem(mp + planes - 1, planes)}
+
+    def remote(src, dst, send, recv_sem, device):
+        return pltpu.make_async_remote_copy(
+            src_ref=src, dst_ref=dst, send_sem=send, recv_sem=recv_sem,
+            device_id=device, device_id_type=pl.DeviceIdType.MESH,
+        )
+
+    def peer(d):
+        return lax.rem(me + d, span)
+
+    barrier = pltpu.get_barrier_semaphore()
+    for axis, here, count in (("span", me, span), ("plane", mp, planes)):
+        for d in range(1, count):
+            pl.semaphore_signal(
+                barrier, inc=1, device_id={axis: lax.rem(here + d, count)},
+                device_id_type=pl.DeviceIdType.MESH,
+            )
+    tables = [
+        pltpu.make_async_copy(inv_hbm, inv, table_sem.at[0]),
+        pltpu.make_async_copy(fwd_hbm, fwd, table_sem.at[1]),
+    ]
+    for copy in tables:
+        copy.start()
+    pack(x_ref, perm_ref, d_ref, blocks, elems)
+    pl.semaphore_wait(barrier, span + planes - 2)
+
+    def state_copy(k, d):
+        src = d_ref.at[peer(d) * chunks + k]
+        return remote(src, recv.at[k, me], s1.at[k, d - 1], r1.at[k, d - 1], {"span": peer(d)})
+
+    def row_copies(k):
+        a = remote(recv.at[k, :, 4 * bl : 5 * bl, :], below.at[k], s2.at[k, 0], r2.at[k, 0], up)
+        b = remote(recv.at[k, :, 0:bl, :], above.at[k], s2.at[k, 1], r2.at[k, 1], down)
+        return a, b
+
+    def tend_copy(k, d):
+        src = tsend.at[k, peer(d)]
+        return remote(src, trecv.at[k, me], s3.at[k, d - 1], r3.at[k, d - 1], {"span": peer(d)})
+
+    def join_copies(n):
+        a = remote(c_ref.at[4], lo.at[n], s4.at[n, 0], r4.at[n, 0], up)
+        b = remote(c_ref.at[0], hi.at[n], s4.at[n, 1], r4.at[n, 1], down)
+        return a, b
+
+    def start_pair(pair):
+        pl.when(beyond)(pair[0].start)
+        pl.when(inner)(pair[1].start)
+
+    def wait_sent(pair):
+        pl.when(beyond)(pair[0].wait_send)
+        pl.when(inner)(pair[1].wait_send)
+
+    def wait_got(pair):
+        pl.when(inner)(pair[0].wait_recv)
+        pl.when(beyond)(pair[1].wait_recv)
+
+    for k in range(chunks):
+        for d in range(1, span):
+            state_copy(k, d).start()
+    for k in range(chunks):
+        recv[k, me] = d_ref[me * chunks + k]
+
+    @pl.when(first)
+    def _():
+        below[...] = jnp.zeros_like(below)
+        lo[...] = jnp.zeros_like(lo)
+
+    @pl.when(last)
+    def _():
+        above[...] = jnp.zeros_like(above)
+        hi[...] = jnp.zeros_like(hi)
+
+    for k in range(chunks):
+        for d in range(1, span):
+            state_copy(k, d).wait_recv()
+        start_pair(row_copies(k))
+        if k == 0:
+            for copy in tables:
+                copy.wait()
+        to_planes([recv.at[k]], inv, fld, 0)
+        wait_got(row_copies(k))
+        to_planes([below.at[k], above.at[k]], inv, fld, sr)
+        outer_rows(fld, tag_ref.at[k], elems, first, last)
+        pointwise(fld, r_ref, h_ref, elems)
+        spectral(r_ref, h_ref, fwd, tsend.at[k])
+        for d in range(1, span):
+            tend_copy(k, d).start()
+        trecv[k, me] = tsend[k, me]
+
+    for k in range(chunks):
+        for d in range(1, span):
+            tend_copy(k, d).wait_recv()
+    column_load(d_ref, trecv, c_ref, elems, (0, 4))
+    start_pair(join_copies(0))
+    column_load(d_ref, trecv, c_ref, elems, (1, 2, 3))
+    shift, theta = shift_ref[...], theta_ref[...]
+    sums = []
+    prev = None
+    for n, v in enumerate((v0, v1, v2)):
+        wait_got(join_copies(n))
+        sums.append(join_rows(c_ref, lo.at[n], hi.at[n], prev, theta, v, first, last))
+        wait_sent(join_copies(n))
+        outer = image(v, c_ref, shift, (0, 4))
+        if n < 2:
+            start_pair(join_copies(n + 1))
+        sums.append(outer + image(v, c_ref, shift, (1, 2, 3)))
+        prev = v
+    rows = [jnp.sum(t, axis=0, keepdims=True) for t in sums]
+    part[...] = jnp.concatenate(rows + [jnp.zeros_like(rows[0])] * 2, axis=0)
+
+    def part_copy(d):
+        to = {"plane": lax.rem(mp + d, planes)}
+        return remote(part, parts.at[mp], s5.at[d - 1], r5.at[d - 1], to)
+
+    for d in range(1, planes):
+        part_copy(d).start()
+    parts[mp] = part[...]
+    for d in range(1, planes):
+        part_copy(d).wait_recv()
+    got = jnp.sum(parts[...], axis=0)
+    n0, h0, n2, h2, n4, h4 = [got[k : k + 1] for k in range(6)]
+    nu = [n0, h0 - theta * n0, n2, h2 - theta * n2, n4, h4 - theta * n4]
+    y = solve3(nu, theta)
+    total = v0.shape[2]
+    for j in range(5):
+        for i in range(4):
+            out_ref[j, i * total : (i + 1) * total, :] = (
+                y[0] * v0[j, i] + y[1] * v1[j, i] + y[2] * v2[j, i]
+            )
+    for k in range(chunks):
+        for d in range(1, span):
+            state_copy(k, d).wait_send()
+            tend_copy(k, d).wait_send()
+        wait_sent(row_copies(k))
+    for d in range(1, planes):
+        part_copy(d).wait_send()
 
 
 def shape(*dims):
@@ -328,100 +475,74 @@
     assert rows == 5
     span, planes = lax.axis_size("span"), lax.axis_size("plane")
     total = cols // 5
-    elems = total // span
-    block = 5 * elems
-    sr, tr = 5 * block + PAD, 20 * elems + PAD
-    my_span, my_plane = lax.axis_index("span"), lax.axis_index("plane")
-    first, last = my_plane == 0, my_plane == planes - 1
-    up = [(i, i + 1) for i in range(planes - 1)]
-    down = [(i + 1, i) for i in range(planes - 1)]
+    mine = total // span
+    chunks = 2 if mine % 16 == 0 else 1
+    elems = mine // chunks
+    bl = 5 * elems
+    sr, tr = 5 * bl + PAD, 20 * elems + PAD
+    my_span = lax.axis_index("span")
 
     inverse, inner, outer = basis_tables()
     inv = jnp.asarray(np.stack(halves(inverse)))
     fwd = jnp.asarray(np.stack(halves(inner) + halves(outer)))
-    perm = jnp.asarray(perm_tables(span, elems))
+    perm = jnp.asarray(perm_tables(span * chunks, elems))
     expand = jnp.asarray(expand_table(total))
     ids = my_span * modes + jnp.arange(modes, dtype=jnp.int32)
     wave = (ids // 2).astype(f32) / KMODES
     shift = (1.0 + STIFF * wave * wave)[None, :]
     theta = 0.6 + 0.254 * (shift - 1.0)
-    tags = jnp.tile(lax.dynamic_slice_in_dim(wall_tag, my_span * elems, elems, 0), 5)[:, None]
-    edge = jnp.stack([first, last]).astype(jnp.int32)
-    smem = pl.BlockSpec(memory_space=pltpu.SMEM)
+    tags = lax.dynamic_slice_in_dim(wall_tag, my_span * mine, mine, 0).reshape(chunks, 1, elems)
+    tags = jnp.tile(tags, (1, 5, 1)).reshape(chunks, bl, 1)
     vmem = pl.BlockSpec(memory_space=pltpu.VMEM)
-
-    own = call(lambda x, p, d: pack(x, p, d, span, elems), shape(span, sr, modes))(state, perm)
-    recv = lax.all_to_all(own, "span", 0, 0, tiled=True)
-    below = lax.ppermute(recv[:, 4 * block : 5 * block], "plane", up)
-    above = lax.ppermute(recv[:, :block], "plane", down)
-
-    def middle(edge_ref, x, lo, hi, tag, inv_ref, fwd_ref, t_ref, fld, r, h):
-        physical(x, lo, hi, tag, inv_ref, fld, elems, edge_ref[0] == 1, edge_ref[1] == 1)
-        pointwise(fld, r, h, elems)
-        spectral(r, h, fwd_ref, t_ref)
-
-    sent = call(
-        middle,
-        shape(span, tr, modes),
-        [
-            pltpu.VMEM((sr + 2 * block, PLANES), f32),
-            pltpu.VMEM((tr, PLANES), f32),
-            pltpu.VMEM((tr, PLANES), f32),
+    hbm = pl.BlockSpec(memory_space=pl.ANY)
+    buf = lambda *d: pltpu.VMEM(d, f32)
+    dma = lambda *d: pltpu.SemaphoreType.DMA(d)
+    joined = buf(5, 4, total, modes)
+    halo = buf(3, 4, total, modes)
+
+    x = pl.pallas_call(
+        functools.partial(segment, (span, planes, chunks, elems)),
+        out_shape=shape(5, 4 * total, modes),
+        in_specs=[vmem] * 5 + [hbm] * 2,
+        out_specs=vmem,
+        scratch_shapes=[
+            pltpu.VMEM(inv.shape, bf16),
+            pltpu.VMEM(fwd.shape, bf16),
+            buf(span * chunks, sr, modes),
+            buf(chunks, span, sr, modes),
+            buf(chunks, span, bl, modes),
+            buf(chunks, span, bl, modes),
+            buf(sr + 2 * bl, PLANES),
+            buf(tr, PLANES),
+            buf(tr, PLANES),
+            buf(chunks, span, tr, modes),
+            buf(chunks, span, tr, modes),
+            joined, joined, joined, joined, halo, halo,
+            buf(8, modes),
+            buf(planes, 8, modes),
+            dma(2),
+            dma(chunks, span - 1), dma(chunks, span - 1),
+            dma(chunks, 2), dma(chunks, 2),
+            dma(chunks, span - 1), dma(chunks, span - 1),
+            dma(3, 2), dma(3, 2),
+            dma(planes - 1), dma(planes - 1),
         ],
-        in_specs=[smem] + [vmem] * 6,
-        out_specs=vmem,
-    )(edge, recv, below, above, tags, inv, fwd)
-    got = lax.all_to_all(sent, "span", 0, 0, tiled=True)
-    joined = shape(5, 4, total, modes)
-    part = call(lambda d, t, c: column_load(d, t, c, elems), joined)(own, got)
-
-    def join(c):
-        return lax.ppermute(c[4], "plane", up), lax.ppermute(c[0], "plane", down)
-
-    def row_join(c, lo, hi, prev, theta_ref, v):
-        for j in range(5):
-            for i in range(4):
-                val = c[j, i]
-                if j == 0:
-                    val = val + lo[i]
-                if j == 4:
-                    val = val + hi[i]
-                if prev is not None:
-                    val = val - theta_ref[...] * prev[j, i]
-                v[j, i] = val
-
-    row = shape(1, modes)
-
-    def step0(edge_ref, c, lo, hi, th, sh, v, out, sq, dt):
-        row_join(c, lo, hi, None, None, v)
-        sq[...] = square_sum(v, edge_ref[0] == 1, edge_ref[1] == 1)
-        dt[...] = apply_local(v, out, sh[...])
-
-    def step1(edge_ref, c, lo, hi, prev, th, sh, v, out, sq, dt):
-        row_join(c, lo, hi, prev, th, v)
-        sq[...] = square_sum(v, edge_ref[0] == 1, edge_ref[1] == 1)
-        dt[...] = apply_local(v, out, sh[...])
-
-    def finish(edge_ref, c, lo, hi, prev, th, sh, v, sq, dt, out):
-        step1(edge_ref, c, lo, hi, prev, th, sh, v, out, sq, dt)
-
-    v0, c1, s0, t0 = call(step0, (joined, joined, row, row), in_specs=[smem] + [vmem] * 5)(
-        edge, part, *join(part), theta, shift
-    )
-    v1, c2, s1, t1 = call(step1, (joined, joined, row, row), in_specs=[smem] + [vmem] * 6)(
-        edge, c1, *join(c1), v0, theta, shift
-    )
-    v2, s2, t2 = call(
-        finish,
-        (joined, row, row),
-        [pltpu.VMEM(joined.shape, f32)],
-        in_specs=[smem] + [vmem] * 6,
-    )(edge, c2, *join(c2), v1, theta, shift)
-    sums = lax.psum(jnp.concatenate([s0, t0, s1, t1, s2, t2], axis=0), "plane")
-    n0, h0, n2, h2, n4, h4 = [sums[k : k + 1] for k in range(6)]
-    nu = [n0, h0 - theta * n0, n2, h2 - theta * n2, n4, h4 - theta * n4]
-    y = jnp.concatenate(solve3(nu, theta), axis=0)
-    return call(unpack, shape(modes, rows, cols))(v0, v1, v2, y, expand)
+        compiler_params=pltpu.CompilerParams(
+            vmem_limit_bytes=VMEM_LIMIT, collective_id=0, has_side_effects=True
+        ),
+    )(state.transpose(1, 0, 2), perm, tags, shift, theta, inv, fwd)
+    out = pl.pallas_call(
+        unpack,
+        out_shape=shape(5, modes, cols),
+        grid=(5,),
+        in_specs=[
+            pl.BlockSpec((1, 4 * total, modes), lambda j: (j, 0, 0)),
+            pl.BlockSpec(expand.shape, lambda j: (0, 0)),
+        ],
+        out_specs=pl.BlockSpec((1, modes, cols), lambda j: (j, 0, 0)),
+        compiler_params=pltpu.CompilerParams(vmem_limit_bytes=VMEM_LIMIT),
+    )(x, expand)
+    return out.transpose(1, 0, 2)
 
 
 def solution(mesh):

time: 154 us -> 75.9 us (0.49)
  blocking collectives: 65.5 us -> 0 us
  Pallas kernels: 38.7 us -> 73.5 us
  starting transfers between devices: 28.9 us -> 0 us
  local copies, waits for them, and re-layouts: 15.5 us -> 1.55 us
  waiting for transfers between devices: 2.56 us -> 0 us
    all_to_all x2 -> x0, blocking collectives: 47.3 us -> none  [the longest x1 26.2 us: on_device(): recv = lax.all_to_all(own, 'span', 0, 0, tiled=True)]
    pallas_call x7 -> x2, Pallas kernels: 38.7 us -> 73.5 us  [the longest x1 68.2 us: on_device(): pl.pallas_call(functools.partial(segment, (span, planes, chunks, elems)),...]
    ppermute x8 -> x0, starting transfers between devices: 28.9 us -> none  [the longest x6 24.6 us: join(): return (lax.ppermute(c[4], 'plane', up), lax.ppermute(c[0], 'plane', down))]
    psum x1 -> x0, blocking collectives: 18.3 us -> none  [on_device(): sums = lax.psum(jnp.concatenate([s0, t0, s1, t1, s2, t2], axis=0), 'plane')]
    unnamed x29 -> x0, local copies, waits for them, and re-layouts: 7.54 us -> none
    pallas_call x1 -> x0, local copies, waits for them, and re-layouts: 3.22 us -> none  [on_device(): return call(unpack, shape(modes, rows, cols))(v0, v1, v2, y, expand)]
    squeeze x3 -> x0, local copies, waits for them, and re-layouts: 3.19 us -> none  [join(): return (lax.ppermute(c[4], 'plane', up), lax.ppermute(c[0], 'plane', down))]
    ppermute x8 -> x0, waiting for transfers between devices: 2.56 us -> none  [the longest x6 2.55 us: join(): return (lax.ppermute(c[4], 'plane', up), lax.ppermute(c[0], 'plane', down))]
  transfers between devices with their start and end apart: 8 -> 0, of which waited for: 3 -> 0; matrix products, arithmetic and copies ran while one was open for 1% -> 0% of each run, Pallas kernels for 0% -> 0%
where the time goes in v1:
time: 75.9 us; the launch traced here: 75.7 us
  Pallas kernels  73.5 us (97%)
  local copies, waits for them, and re-layouts  1.55 us (2%)
    pallas_call x1, Pallas kernels, on_device(): pl.pallas_call(functools.partial(segment, (span, planes, chunks, elems)),...  68.2 us
    pallas_call x1, Pallas kernels, on_device(): pl.pallas_call(unpack, out_shape=shape(5, modes, cols), grid=(5,), in_spe...  5.29 us

profile of v1, /device:TPU:0, one launch (start us, length us, event | category | flops | bytes accessed | tf_op | source)
XLA Modules:
  0.0 75.7 jit_solution(9619201137506294782)
XLA Ops:
  0.0 0.7 dynamic_slice.3
  0.7 0.1 tile.9
  0.8 0.6 multiply_add_fusion
  1.4 0.7 tile.12.tag_ref
  2.1 68.2 %shard_map.64.x_ref = f32[5,512,128]{2,1,0:T(8,128)} custom-call(f32[5,128,640]{2,1,0:T(8,128)} %bitcast.4, bf16[8,80,256]{2,1,0:T(8,128)(2,1)} %constant.49.clone.perm_ref, s32[2,80,1]{2,1,0:T(8,128)} %tile.12.tag_ref, f32[1,128]{1,0:T(1,128)} %get-tuple-element.6.shift_ref, f32[1,128]{1,0:T(1,128)} %get-tuple-element.5.theta_ref, ...), custom_call_target="tpu_custom_call" | custom-call | tf_op jit(solution)/shard_map/pallas_call | solution.py:503
  70.4 5.3 %shard_map.65 = f32[5,128,640]{2,1,0:T(8,128)} custom-call(f32[5,512,128]{2,1,0:T(8,128)} %shard_map.64.x_ref, bf16[512,640]{1,0:T(8,128)(2,1)} %constant.50.clone.exp_ref), custom_call_target="tpu_custom_call" | custom-call | tf_op jit(solution)/shard_map/pallas_call | solution.py:534
  (1 shorter events, 0.0 us)

commit v2 on v1

--- a/solution.py
+++ b/solution.py
@@ -91,37 +91,44 @@
     return pltpu.roll(x, by % x.shape[0], 0)
 
 
-def pack(x_ref, perm_ref, d_ref, span, elems):
+def pack(x_ref, perm_ref, d_ref, span, chunks, elems):
     rows, modes, cols = x_ref.shape
     block = 5 * elems
+    wide = block * chunks
+    blocks = span * chunks
     parts = split2(x_ref[...].reshape(rows * modes, cols))
     for s in range(span):
-        lo = block * s // 128 * 128
-        hi = -(-block * (s + 1) // 128) * 128
+        lo = wide * s // 128 * 128
+        hi = -(-wide * (s + 1) // 128) * 128
         perm = perm_ref[s, :, : hi - lo]
         got = sum(dot(perm, part[:, lo:hi], NT) for part in parts)
-        for j in range(rows):
-            d_ref[s, block * j : block * (j + 1), :] = got[:, modes * j : modes * (j + 1)]
-    for s in range(span):
-        left, right = (s - 1) % span, (s + 1) % span
+        for k in range(chunks):
+            for j in range(rows):
+                d_ref[s * chunks + k, block * j : block * (j + 1), :] = got[
+                    block * k : block * (k + 1), modes * j : modes * (j + 1)
+                ]
+    for b in range(blocks):
+        left, right = (b - 1) % blocks, (b + 1) % blocks
         for j in range(rows):
             at = block * rows + 2 * j
             last = block * j + block - 1
-            d_ref[s, at : at + 1, :] = d_ref[left, last : last + 1, :]
-            d_ref[s, at + 1 : at + 2, :] = d_ref[right, block * j : block * j + 1, :]
-        for at in range(block * rows + 2 * rows, block * rows + PAD):
-            d_ref[s, at : at + 1, :] = jnp.zeros((1, modes), f32)
-
-
-def perm_tables(span, elems):
-    block = 5 * elems
-    width = max(-(-block * (s + 1) // 128) * 128 - block * s // 128 * 128 for s in range(span))
-    perm = np.zeros((span, block, width), np.float32)
+            d_ref[b, at : at + 1, :] = d_ref[left, last : last + 1, :]
+            d_ref[b, at + 1 : at + 2, :] = d_ref[right, block * j : block * j + 1, :]
+        at = block * rows + 2 * rows
+        d_ref[b, at : block * rows + PAD, :] = jnp.zeros((PAD - 2 * rows, modes), f32)
+
+
+def perm_tables(span, chunks, elems):
+    wide = 5 * elems * chunks
+    width = max(-(-wide * (s + 1) // 128) * 128 - wide * s // 128 * 128 for s in range(span))
+    perm = np.zeros((span, wide, width), np.float32)
     for s in range(span):
-        lo = block * s // 128 * 128
-        for i in range(5):
-            for e in range(elems):
-                perm[s, i * elems + e, block * s + 5 * e + i - lo] = 1.0
+        lo = wide * s // 128 * 128
+        for k in range(chunks):
+            for i in range(5):
+                for e in range(elems):
+                    row = (k * 5 + i) * elems + e
+                    perm[s, row, wide * s + 5 * (k * elems + e) + i - lo] = 1.0
     return perm.astype(bf16)
 
 
@@ -136,14 +143,14 @@
         fld_ref[lo : lo + x.shape[0], at] = dot(high, bh) + dot(high, bl) + dot(low, bh)
 
 
-def outer_rows(fld_ref, tag_ref, elems, first, last):
+def outer_rows(fld_ref, tag, elems, first, last):
     block = 5 * elems
     sr = 5 * block + PAD
 
     @pl.when(first)
     def _():
         own = fld_ref[0:block, :]
-        fld_ref[sr : sr + block, :] = jnp.where(tag_ref[...] == 1, -own, own)
+        fld_ref[sr : sr + block, :] = jnp.where(tag == 1, -own, own)
 
     @pl.when(last)
     def _():
@@ -203,7 +210,7 @@
     lax.fori_loop(0, PLANES // lane, body, 0)
 
 
-def spectral(r_ref, h_ref, fwd_ref, t_ref):
+def spectral(r_ref, h_ref, fwd_ref, t_ref, send):
     span, _, modes = t_ref.shape
     rh, rl = split2(r_ref[...])
     hh, hl = split2(h_ref[...])
@@ -214,7 +221,9 @@
         c, d = fwd_ref[2, :, at], fwd_ref[3, :, at]
         t = dot(rh, a) + dot(rl, a) + dot(rh, b) + dot(hh, c) + dot(hl, c) + dot(hh, d)
         for k in range(step // modes):
-            t_ref[n * (step // modes) + k] = t[:, modes * k : modes * (k + 1)]
+            s = n * (step // modes) + k
+            t_ref[s] = t[:, modes * k : modes * (k + 1)]
+            send(s)
 
 
 def column_load(d_ref, t_ref, c_ref, elems, js):
@@ -246,8 +255,10 @@
     return jnp.sum(x.reshape(x.shape[0] // 8, 8, x.shape[1]), axis=0)
 
 
-def image(v_ref, out_ref, shift, js):
-    col = [2.0 * WEIGHT[0], WEIGHT[1], WEIGHT[2], WEIGHT[3]]
+COLW = [2.0 * WEIGHT[0], WEIGHT[1], WEIGHT[2], WEIGHT[3]]
+
+
+def stretch(v_ref, out_ref, js):
     for j in js:
         a = [v_ref[j, i] for i in range(4)]
         a.append(roll(a[0], -1))
@@ -255,20 +266,23 @@
         kx[0] = kx[0] + roll(kx[4], 1)
         for i in range(4):
             out_ref[j, i] = kx[i]
+
+
+def image(v_ref, out_ref, shift, js):
     total = 0.0
     for i in range(4):
         a = [v_ref[j, i] for j in range(5)]
-        ky = along(KMAT * (VISCOUS * col[i]), a, 1)
+        ky = along(KMAT * (VISCOUS * COLW[i]), a, 1)
         for j in js:
-            val = out_ref[j, i] + ky[j] + (shift * float(WEIGHT[j] * col[i])) * a[j]
+            val = out_ref[j, i] + ky[j] + (shift * float(WEIGHT[j] * COLW[i])) * a[j]
             out_ref[j, i] = val
             total = total + fold(val * a[j])
     return total
 
 
-def join_rows(c_ref, lo, hi, prev, theta, v_ref, first, last):
+def join_rows(c_ref, lo, hi, prev, theta, v_ref, first, last, js):
     total = 0.0
-    for j in (0, 4, 1, 2, 3):
+    for j in js:
         part = 0.0
         for i in range(4):
             val = c_ref[j, i]
@@ -303,8 +317,11 @@
     return z0 / a[0][0] - l10 * y1 - l20 * y2, y1, y2
 
 
-def unpack(x_ref, exp_ref, out_ref):
-    out_ref[0] = sum(dot(part, exp_ref[...], TN) for part in split2(x_ref[0]))
+def unpack(v_ref, exp_ref, out_ref):
+    rows, four, total, modes = v_ref.shape
+    x = jnp.concatenate([v_ref[j].reshape(four * total, modes) for j in range(rows)], axis=1)
+    full = sum(dot(part, exp_ref[...], TN) for part in split2(x))
+    out_ref[...] = full.reshape(out_ref.shape)
 
 
 def expand_table(total):
@@ -316,13 +333,13 @@
 
 
 def segment(
-    dims, x_ref, perm_ref, tag_ref, shift_ref, theta_ref, inv_hbm, fwd_hbm, out_ref,
-    inv, fwd, d_ref, recv, below, above, fld, r_ref, h_ref, tsend, trecv,
+    dims, x_ref, perm_ref, tag_ref, inv_hbm, fwd_hbm, exp_hbm, out_ref,
+    inv, fwd, expand, w0, w1, w2, d_ref, recv, below, above, fld, r_ref, h_ref, tsend, trecv,
     c_ref, v0, v1, v2, lo, hi, part, parts,
     table_sem, s1, r1, s2, r2, s3, r3, s4, r4, s5, r5,
 ):
     span, planes, chunks, elems = dims
-    blocks, bl = span * chunks, 5 * elems
+    modes, bl = x_ref.shape[1], 5 * elems
     sr = 5 * bl + PAD
     me, mp = lax.axis_index("span"), lax.axis_index("plane")
     first, last = mp == 0, mp == planes - 1
@@ -348,10 +365,11 @@
     tables = [
         pltpu.make_async_copy(inv_hbm, inv, table_sem.at[0]),
         pltpu.make_async_copy(fwd_hbm, fwd, table_sem.at[1]),
+        pltpu.make_async_copy(exp_hbm, expand, table_sem.at[2]),
     ]
     for copy in tables:
         copy.start()
-    pack(x_ref, perm_ref, d_ref, blocks, elems)
+    pack(x_ref, perm_ref, d_ref, span, chunks, elems)
     pl.semaphore_wait(barrier, span + planes - 2)
 
     def state_copy(k, d):
@@ -366,6 +384,22 @@
     def tend_copy(k, d):
         src = tsend.at[k, peer(d)]
         return remote(src, trecv.at[k, me], s3.at[k, d - 1], r3.at[k, d - 1], {"span": peer(d)})
+
+    def tend_start(k, s):
+        off = lax.rem(s - me + span, span)
+
+        @pl.when(off > 0)
+        def _():
+            remote(
+                tsend.at[k, s], trecv.at[k, me], s3.at[k, off - 1], r3.at[k, off - 1], {"span": s}
+            ).start()
+
+    def tags(k):
+        total = tag_ref.shape[1]
+        element = lax.broadcasted_iota(jnp.int32, (elems, total), 0) + (me * chunks + k) * elems
+        lane = lax.broadcasted_iota(jnp.int32, (elems, total), 1)
+        column = jnp.sum(jnp.where(element == lane, tag_ref[...], 0), axis=1, keepdims=True)
+        return jnp.concatenate([column] * 5, axis=0)
 
     def join_copies(n):
         a = remote(c_ref.at[4], lo.at[n], s4.at[n, 0], r4.at[n, 0], up)
@@ -410,11 +444,9 @@
         to_planes([recv.at[k]], inv, fld, 0)
         wait_got(row_copies(k))
         to_planes([below.at[k], above.at[k]], inv, fld, sr)
-        outer_rows(fld, tag_ref.at[k], elems, first, last)
+        outer_rows(fld, tags(k), elems, first, last)
         pointwise(fld, r_ref, h_ref, elems)
-        spectral(r_ref, h_ref, fwd, tsend.at[k])
-        for d in range(1, span):
-            tend_copy(k, d).start()
+        spectral(r_ref, h_ref, fwd, tsend.at[k], functools.partial(tend_start, k))
         trecv[k, me] = tsend[k, me]
 
     for k in range(chunks):
@@ -423,17 +455,28 @@
     column_load(d_ref, trecv, c_ref, elems, (0, 4))
     start_pair(join_copies(0))
     column_load(d_ref, trecv, c_ref, elems, (1, 2, 3))
-    shift, theta = shift_ref[...], theta_ref[...]
+    ids = me * modes + lax.broadcasted_iota(jnp.int32, (1, modes), 1)
+    wave = lax.shift_right_logical(ids, 1).astype(f32) / KMODES
+    shift = 1.0 + STIFF * wave * wave
+    theta = 0.6 + 0.254 * (shift - 1.0)
     sums = []
     prev = None
-    for n, v in enumerate((v0, v1, v2)):
+    for n, (v, w) in enumerate(((v0, w0), (v1, w1), (v2, w2))):
+        join = functools.partial(
+            join_rows, c_ref, lo.at[n], hi.at[n], prev, theta, v, first, last
+        )
+        square = join((1, 2, 3))
+        stretch(v, c_ref, (1, 2, 3))
         wait_got(join_copies(n))
-        sums.append(join_rows(c_ref, lo.at[n], hi.at[n], prev, theta, v, first, last))
+        sums.append(square + join((0, 4)))
         wait_sent(join_copies(n))
+        stretch(v, c_ref, (0, 4))
         outer = image(v, c_ref, shift, (0, 4))
         if n < 2:
             start_pair(join_copies(n + 1))
         sums.append(outer + image(v, c_ref, shift, (1, 2, 3)))
+        if n < 2:
+            unpack(v, expand, w)
         prev = v
     rows = [jnp.sum(t, axis=0, keepdims=True) for t in sums]
     part[...] = jnp.concatenate(rows + [jnp.zeros_like(rows[0])] * 2, axis=0)
@@ -445,18 +488,17 @@
     for d in range(1, planes):
         part_copy(d).start()
     parts[mp] = part[...]
+    unpack(v2, expand, w2)
     for d in range(1, planes):
         part_copy(d).wait_recv()
     got = jnp.sum(parts[...], axis=0)
     n0, h0, n2, h2, n4, h4 = [got[k : k + 1] for k in range(6)]
     nu = [n0, h0 - theta * n0, n2, h2 - theta * n2, n4, h4 - theta * n4]
     y = solve3(nu, theta)
-    total = v0.shape[2]
+    y = jnp.concatenate(list(y) + [jnp.zeros_like(y[0])] * 5, axis=0).T
+    y0, y1, y2 = y[:, 0:1], y[:, 1:2], y[:, 2:3]
     for j in range(5):
-        for i in range(4):
-            out_ref[j, i * total : (i + 1) * total, :] = (
-                y[0] * v0[j, i] + y[1] * v1[j, i] + y[2] * v2[j, i]
-            )
+        out_ref[j] = y0 * w0[j] + y1 * w1[j] + y2 * w2[j]
     for k in range(chunks):
         for d in range(1, span):
             state_copy(k, d).wait_send()
@@ -476,23 +518,15 @@
     span, planes = lax.axis_size("span"), lax.axis_size("plane")
     total = cols // 5
     mine = total // span
-    chunks = 2 if mine % 16 == 0 else 1
+    chunks = mine // 8
     elems = mine // chunks
     bl = 5 * elems
     sr, tr = 5 * bl + PAD, 20 * elems + PAD
-    my_span = lax.axis_index("span")
-
     inverse, inner, outer = basis_tables()
     inv = jnp.asarray(np.stack(halves(inverse)))
     fwd = jnp.asarray(np.stack(halves(inner) + halves(outer)))
-    perm = jnp.asarray(perm_tables(span * chunks, elems))
+    perm = jnp.asarray(perm_tables(span, chunks, elems))
     expand = jnp.asarray(expand_table(total))
-    ids = my_span * modes + jnp.arange(modes, dtype=jnp.int32)
-    wave = (ids // 2).astype(f32) / KMODES
-    shift = (1.0 + STIFF * wave * wave)[None, :]
-    theta = 0.6 + 0.254 * (shift - 1.0)
-    tags = lax.dynamic_slice_in_dim(wall_tag, my_span * mine, mine, 0).reshape(chunks, 1, elems)
-    tags = jnp.tile(tags, (1, 5, 1)).reshape(chunks, bl, 1)
     vmem = pl.BlockSpec(memory_space=pltpu.VMEM)
     hbm = pl.BlockSpec(memory_space=pl.ANY)
     buf = lambda *d: pltpu.VMEM(d, f32)
@@ -500,14 +534,16 @@
     joined = buf(5, 4, total, modes)
     halo = buf(3, 4, total, modes)
 
-    x = pl.pallas_call(
+    out = pl.pallas_call(
         functools.partial(segment, (span, planes, chunks, elems)),
-        out_shape=shape(5, 4 * total, modes),
-        in_specs=[vmem] * 5 + [hbm] * 2,
+        out_shape=shape(5, modes, cols),
+        in_specs=[vmem] * 3 + [hbm] * 3,
         out_specs=vmem,
         scratch_shapes=[
             pltpu.VMEM(inv.shape, bf16),
             pltpu.VMEM(fwd.shape, bf16),
+            pltpu.VMEM(expand.shape, bf16),
+            buf(5, modes, cols), buf(5, modes, cols), buf(5, modes, cols),
             buf(span * chunks, sr, modes),
             buf(chunks, span, sr, modes),
             buf(chunks, span, bl, modes),
@@ -520,7 +556,7 @@
             joined, joined, joined, joined, halo, halo,
             buf(8, modes),
             buf(planes, 8, modes),
-            dma(2),
+            dma(3),
             dma(chunks, span - 1), dma(chunks, span - 1),
             dma(chunks, 2), dma(chunks, 2),
             dma(chunks, span - 1), dma(chunks, span - 1),
@@ -530,18 +566,7 @@
         compiler_params=pltpu.CompilerParams(
             vmem_limit_bytes=VMEM_LIMIT, collective_id=0, has_side_effects=True
         ),
-    )(state.transpose(1, 0, 2), perm, tags, shift, theta, inv, fwd)
-    out = pl.pallas_call(
-        unpack,
-        out_shape=shape(5, modes, cols),
-        grid=(5,),
-        in_specs=[
-            pl.BlockSpec((1, 4 * total, modes), lambda j: (j, 0, 0)),
-            pl.BlockSpec(expand.shape, lambda j: (0, 0)),
-        ],
-        out_specs=pl.BlockSpec((1, modes, cols), lambda j: (j, 0, 0)),
-        compiler_params=pltpu.CompilerParams(vmem_limit_bytes=VMEM_LIMIT),
-    )(x, expand)
+    )(state.transpose(1, 0, 2), perm, wall_tag.reshape(1, total), inv, fwd, expand)
     return out.transpose(1, 0, 2)
 
 

time: 75.9 us -> 70 us (0.922)
  Pallas kernels: 73.5 us -> 67.1 us
  local copies, waits for them, and re-layouts: 1.55 us -> 2.71 us
    pallas_call x1 -> x0, Pallas kernels: 5.29 us -> none  [on_device(): pl.pallas_call(unpack, out_shape=shape(5, modes, cols), grid=(5,), in_spe...]
    unnamed x0 -> x1, local copies, waits for them, and re-layouts: none -> 2.71 us
    pallas_call x1, Pallas kernels: 68.2 us -> 67.1 us  [on_device(): pl.pallas_call(functools.partial(segment, (span, planes, chunks, elems)),...]
    another operation x3 -> x0, local copies, waits for them, and re-layouts: 0.82 us -> none  [on_device(): tags = jnp.tile(tags, (1, 5, 1)).reshape(chunks, bl, 1)]
where the time goes in v2:
time: 70 us; the launch traced here: 69.8 us
  Pallas kernels  67.1 us (96%)
  local copies, waits for them, and re-layouts  2.71 us (4%)
    pallas_call x1, Pallas kernels, on_device(): pl.pallas_call(functools.partial(segment, (span, planes, chunks, elems)),...  67.1 us
    unnamed x1, local copies, waits for them, and re-layouts  2.71 us

profile of v2, /device:TPU:0, one launch (start us, length us, event | category | flops | bytes accessed | tf_op | source)
XLA Modules:
  0.0 69.8 jit_solution(15911363241631398925)
XLA Ops:
  0.0 67.1 %shard_map.64 = f32[5,128,640]{2,1,0:T(8,128)} custom-call(f32[5,128,640]{2,1,0:T(8,128)} %bitcast.4, bf16[4,160,256]{2,1,0:T(8,128)(2,1)} %constant.10.clone.perm_ref, s32[1,128]{1,0:T(1,128)} %bitcast.5, bf16[2,512,768]{2,1,0:T(8,128)(2,1)} %constant.8.clone.inv_hbm, bf16[4,768,512]{2,1,0:T(8,128)(2,1)} %constant.9.clone.fwd_hbm, ...), custom_call_target="tpu_custom_call" | custom-call | tf_op jit(solution)/shard_map/pallas_call | solution.py:537
  67.1 2.7 %copy.8 = f32[128,5,640]{2,0,1:T(8,128)} copy(f32[128,5,640]{2,0,1:T(8,128)} %bitcast.3) | data formatting | bytes 3276800

commit v3 on v2

--- a/solution.py
+++ b/solution.py
@@ -14,7 +14,6 @@
 STEP = 0.03
 VISCOUS = 0.05
 STIFF = 4.0
-PAD = 16
 
 f32 = jnp.float32
 bf16 = jnp.bfloat16
@@ -91,7 +90,7 @@
     return pltpu.roll(x, by % x.shape[0], 0)
 
 
-def pack(x_ref, perm_ref, d_ref, span, chunks, elems):
+def pack(x_ref, perm_ref, d_ref, halo_ref, span, chunks, elems, ready):
     rows, modes, cols = x_ref.shape
     block = 5 * elems
     wide = block * chunks
@@ -107,15 +106,18 @@
                 d_ref[s * chunks + k, block * j : block * (j + 1), :] = got[
                     block * k : block * (k + 1), modes * j : modes * (j + 1)
                 ]
-    for b in range(blocks):
-        left, right = (b - 1) % blocks, (b + 1) % blocks
+        ready(s)
+    for s in range(span):
+        left = (s * chunks - 1) % blocks
         for j in range(rows):
-            at = block * rows + 2 * j
             last = block * j + block - 1
-            d_ref[b, at : at + 1, :] = d_ref[left, last : last + 1, :]
-            d_ref[b, at + 1 : at + 2, :] = d_ref[right, block * j : block * j + 1, :]
-        at = block * rows + 2 * rows
-        d_ref[b, at : block * rows + PAD, :] = jnp.zeros((PAD - 2 * rows, modes), f32)
+            halo_ref[s, j : j + 1, :] = d_ref[left, last : last + 1, :]
+            for k in range(chunks):
+                right = (s * chunks + k + 1) % blocks
+                at = rows * (k + 1) + j
+                halo_ref[s, at : at + 1, :] = d_ref[right, block * j : block * j + 1, :]
+        used = rows * (chunks + 1)
+        halo_ref[s, used:, :] = jnp.zeros((halo_ref.shape[1] - used, modes), f32)
 
 
 def perm_tables(span, chunks, elems):
@@ -145,7 +147,7 @@
 
 def outer_rows(fld_ref, tag, elems, first, last):
     block = 5 * elems
-    sr = 5 * block + PAD
+    sr = 5 * block
 
     @pl.when(first)
     def _():
@@ -157,18 +159,21 @@
         fld_ref[sr + block : sr + 2 * block, :] = fld_ref[4 * block : 5 * block, :]
 
 
-def pointwise(fld_ref, r_ref, h_ref, elems):
+def pointwise(fld_ref, halo_ref, edge_ref, carry_ref, r_ref, h_ref, elems, k, chunks):
     block = 5 * elems
-    sr = 5 * block + PAD
+    sr = 5 * block
     lane = 128
+    place = {0: 0, 4: 4 * elems}
+    for j in (1, 2, 3):
+        place[j] = 4 * elems * (j + 1) + 8
     third = DIFF * (-1.0 / 3.0)
 
     def body(n, _):
         at = pl.ds(pl.multiple_of(n * lane, lane), lane)
         row = lax.broadcasted_iota(jnp.int32, (elems, lane), 0)
 
-        def load(k):
-            return fld_ref[k : k + elems, at]
+        def load(base):
+            return fld_ref[base : base + elems, at]
 
         u = [[load(block * j + elems * i) for i in range(5)] for j in range(5)]
         q = [[v * v for v in r] for r in u]
@@ -178,8 +183,9 @@
             dq = along(third, q[j], -1)
             for i in range(5):
                 rhs[j][i] = dq[i] + u[j][i] * du[i]
-            hl = fld_ref[5 * block + 2 * j : 5 * block + 2 * j + 1, at]
-            hr = fld_ref[5 * block + 2 * j + 1 : 5 * block + 2 * j + 2, at]
+            hl = halo_ref[j : j + 1, at] if k == 0 else edge_ref[j : j + 1, at]
+            hr = halo_ref[5 * (k + 1) + j : 5 * (k + 1) + j + 1, at]
+            edge_ref[j : j + 1, at] = u[j][4][elems - 1 : elems, :]
             left = jnp.where(row == 0, hl, roll(u[j][4], 1))
             right = jnp.where(row == elems - 1, hr, roll(u[j][0], -1))
             rhs[j][0] += two_point10(left, u[j][0], left * left, q[j][0]) - 5.0 * q[j][0]
@@ -194,17 +200,25 @@
             upper = load(sr + block + elems * i)
             rhs[0][i] += two_point10(lower, ui[0], lower * lower, qi[0]) - 5.0 * qi[0]
             rhs[4][i] -= two_point10(ui[4], upper, qi[4], upper * upper) - 5.0 * qi[4]
-        for ref, val, scale in ((r_ref, rhs, None), (h_ref, q, 0.5)):
-            for j in range(5):
+        for ref, val, scale, base in ((r_ref, rhs, None, 0), (h_ref, q, 0.5, 5)):
+            for n, j in enumerate((0, 4, 1, 2, 3)):
                 a = val[j] if scale is None else [scale * v for v in val[j]]
-                ref[4 * elems * j : 4 * elems * j + elems, at] = a[0] + jnp.where(
-                    row == 0, 0.0, roll(a[4], 1)
+                kept = 0.0 if k == 0 else carry_ref[base + j : base + j + 1, at]
+                ref[place[j] : place[j] + elems, at] = a[0] + jnp.where(
+                    row == 0, kept, roll(a[4], 1)
                 )
                 for i in (1, 2, 3):
-                    k = elems * (4 * j + i)
-                    ref[k : k + elems, at] = a[i]
-                ref[20 * elems + j : 20 * elems + j + 1, at] = a[4][elems - 1 : elems, :]
-            ref[20 * elems + 5 : 20 * elems + PAD, at] = jnp.zeros((PAD - 5, lane), f32)
+                    to = place[j] + elems * i
+                    ref[to : to + elems, at] = a[i]
+                tail = a[4][elems - 1 : elems, :]
+                if k == chunks - 1:
+                    ref[8 * elems + n : 8 * elems + n + 1, at] = tail
+                else:
+                    carry_ref[base + j : base + j + 1, at] = tail
+            if k == chunks - 1:
+                ref[8 * elems + 5 : 8 * elems + 8, at] = jnp.zeros((3, lane), f32)
+            else:
+                ref[8 * elems : 8 * elems + 8, at] = jnp.zeros((8, lane), f32)
         return 0
 
     lax.fori_loop(0, PLANES // lane, body, 0)
@@ -226,29 +240,41 @@
             send(s)
 
 
-def column_load(d_ref, t_ref, c_ref, elems, js):
-    chunks, span, _, modes = t_ref.shape
-    blocks = chunks * span
+def column_load(d_ref, c_ref, elems, js):
+    blocks, _, modes = d_ref.shape
     block = 5 * elems
     row = lax.broadcasted_iota(jnp.int32, (elems, modes), 0)
     for j in js:
         for b in range(blocks):
-            s, k = divmod(b, chunks)
             left = (b - 1) % blocks
-            sl, kl = divmod(left, chunks)
             for i in range(4):
                 at = block * j + elems * i
-                tat = elems * (4 * j + i)
-                val = d_ref[b, at : at + elems, :] + t_ref[k, s, tat : tat + elems, :]
+                val = d_ref[b, at : at + elems, :]
                 if i == 0:
                     at4 = block * j + 4 * elems
-                    extra = 20 * elems + j
-                    edge = (
-                        d_ref[left, at4 + elems - 1 : at4 + elems, :]
-                        + t_ref[kl, sl, extra : extra + 1, :]
-                    )
+                    edge = d_ref[left, at4 + elems - 1 : at4 + elems, :]
                     val += jnp.where(row == 0, edge, roll(d_ref[b, at4 : at4 + elems, :], 1))
                 c_ref[j, i, elems * b : elems * (b + 1), :] = val * float(WEIGHT[j] * WEIGHT[i])
+
+
+def add_tendency(v_ref, t_ref, elems, k, chunks):
+    span = t_ref.shape[1]
+    for j in range(5):
+        base = {0: 0, 4: 4 * elems}.get(j, 4 * elems * (j + 1) + 8)
+        for s in range(span):
+            at = slice(elems * (s * chunks + k), elems * (s * chunks + k + 1))
+            for i in range(4):
+                part = t_ref[k, s, base + elems * i : base + elems * (i + 1), :]
+                v_ref[j, i, at, :] += part * float(WEIGHT[j] * WEIGHT[i])
+
+
+def add_ends(v_ref, t_ref, elems, chunks):
+    span = t_ref.shape[1]
+    for n, j in enumerate((0, 4, 1, 2, 3)):
+        for s in range(span):
+            end = t_ref[chunks - 1, (s - 1) % span, 8 * elems + n : 8 * elems + n + 1, :]
+            at = elems * s * chunks
+            v_ref[j, 0, at : at + 1, :] += end * float(WEIGHT[j] * WEIGHT[0])
 
 
 def fold(x):
@@ -280,10 +306,8 @@
     return total
 
 
-def join_rows(c_ref, lo, hi, prev, theta, v_ref, first, last, js):
-    total = 0.0
+def join_rows(c_ref, lo, hi, prev, theta, v_ref, js):
     for j in js:
-        part = 0.0
         for i in range(4):
             val = c_ref[j, i]
             if j == 0:
@@ -293,7 +317,12 @@
             if prev is not None:
                 val = val - theta * prev[j, i]
             v_ref[j, i] = val
-            part = part + fold(val * val)
+
+
+def squares(v_ref, first, last, js):
+    total = 0.0
+    for j in js:
+        part = sum(fold(v_ref[j, i] * v_ref[j, i]) for i in range(4))
         if j == 0:
             part = part * jnp.where(first, 1.0, 0.5)
         if j == 4:
@@ -334,13 +363,13 @@
 
 def segment(
     dims, x_ref, perm_ref, tag_ref, inv_hbm, fwd_hbm, exp_hbm, out_ref,
-    inv, fwd, expand, w0, w1, w2, d_ref, recv, below, above, fld, r_ref, h_ref, tsend, trecv,
-    c_ref, v0, v1, v2, lo, hi, part, parts,
-    table_sem, s1, r1, s2, r2, s3, r3, s4, r4, s5, r5,
+    inv, fwd, expand, w0, w1, w2, d_ref, dh, recv, hrecv, below, above, fld, halo, edge, carry,
+    r_ref, h_ref, tsend, zlo, zhi, tjoin, trecv, c_ref, v0, v1, v2, lo, hi, part, parts,
+    table_sem, s1, r1, sh, rh, s2, r2, sz, rz, s3, r3, s6, r6, s4, r4, s5, r5,
 ):
     span, planes, chunks, elems = dims
     modes, bl = x_ref.shape[1], 5 * elems
-    sr = 5 * bl + PAD
+    sr, ab = 5 * bl, 8 * elems
     me, mp = lax.axis_index("span"), lax.axis_index("plane")
     first, last = mp == 0, mp == planes - 1
     inner, beyond = mp > 0, mp < planes - 1
@@ -369,30 +398,47 @@
     ]
     for copy in tables:
         copy.start()
-    pack(x_ref, perm_ref, d_ref, span, chunks, elems)
-    pl.semaphore_wait(barrier, span + planes - 2)
-
-    def state_copy(k, d):
-        src = d_ref.at[peer(d) * chunks + k]
-        return remote(src, recv.at[k, me], s1.at[k, d - 1], r1.at[k, d - 1], {"span": peer(d)})
+
+    def to_span(s, start):
+        off = lax.rem(s - me + span, span)
+        pl.when(off > 0)(lambda: start(off - 1))
+
+    def state_copy(k, s, n):
+        src = d_ref.at[s * chunks + k]
+        return remote(src, recv.at[k, me], s1.at[k, n], r1.at[k, n], {"span": s})
+
+    def halo_copy(s, n):
+        return remote(dh.at[s], hrecv.at[me], sh.at[n], rh.at[n], {"span": s})
 
     def row_copies(k):
         a = remote(recv.at[k, :, 4 * bl : 5 * bl, :], below.at[k], s2.at[k, 0], r2.at[k, 0], up)
         b = remote(recv.at[k, :, 0:bl, :], above.at[k], s2.at[k, 1], r2.at[k, 1], down)
         return a, b
 
-    def tend_copy(k, d):
-        src = tsend.at[k, peer(d)]
-        return remote(src, trecv.at[k, me], s3.at[k, d - 1], r3.at[k, d - 1], {"span": peer(d)})
-
-    def tend_start(k, s):
-        off = lax.rem(s - me + span, span)
-
-        @pl.when(off > 0)
-        def _():
-            remote(
-                tsend.at[k, s], trecv.at[k, me], s3.at[k, off - 1], r3.at[k, off - 1], {"span": s}
-            ).start()
+    def shared_copies(k):
+        src = tsend.at[k, :, 0 : ab + 8, :]
+        a = remote(src, zlo.at[k], sz.at[k, 0], rz.at[k, 0], up)
+        b = remote(src, zhi.at[k], sz.at[k, 1], rz.at[k, 1], down)
+        return a, b
+
+    def inner_copy(k, s, n):
+        rows = slice(ab + 8, 20 * elems + 8)
+        src, dst = tsend.at[k, s, rows, :], trecv.at[k, me, rows, :]
+        return remote(src, dst, s3.at[k, n], r3.at[k, n], {"span": s})
+
+    def outer_copy(k, s, n):
+        rows = slice(0, ab + 8 if k == chunks - 1 else ab)
+        src, dst = tjoin.at[k, s, rows, :], trecv.at[k, me, rows, :]
+        return remote(src, dst, s6.at[k, n], r6.at[k, n], {"span": s})
+
+    def join_copies(n):
+        a = remote(c_ref.at[4], lo.at[n], s4.at[n, 0], r4.at[n, 0], up)
+        b = remote(c_ref.at[0], hi.at[n], s4.at[n, 1], r4.at[n, 1], down)
+        return a, b
+
+    def part_copy(d):
+        to = {"plane": lax.rem(mp + d, planes)}
+        return remote(part, parts.at[mp], s5.at[d - 1], r5.at[d - 1], to)
 
     def tags(k):
         total = tag_ref.shape[1]
@@ -401,11 +447,6 @@
         column = jnp.sum(jnp.where(element == lane, tag_ref[...], 0), axis=1, keepdims=True)
         return jnp.concatenate([column] * 5, axis=0)
 
-    def join_copies(n):
-        a = remote(c_ref.at[4], lo.at[n], s4.at[n, 0], r4.at[n, 0], up)
-        b = remote(c_ref.at[0], hi.at[n], s4.at[n, 1], r4.at[n, 1], down)
-        return a, b
-
     def start_pair(pair):
         pl.when(beyond)(pair[0].start)
         pl.when(inner)(pair[1].start)
@@ -418,43 +459,93 @@
         pl.when(inner)(pair[0].wait_recv)
         pl.when(beyond)(pair[1].wait_recv)
 
-    for k in range(chunks):
-        for d in range(1, span):
-            state_copy(k, d).start()
+    def ready(s):
+        if s == 0:
+            pl.semaphore_wait(barrier, span + planes - 2)
+        to_span(s, lambda n: state_copy(0, s, n).start())
+
+    pack(x_ref, perm_ref, d_ref, dh, span, chunks, elems, ready)
+    for s in range(span):
+        to_span(s, lambda n: halo_copy(s, n).start())
+    for k in range(1, chunks):
+        for s in range(span):
+            to_span(s, lambda n: state_copy(k, s, n).start())
+    column_load(d_ref, c_ref, elems, (0, 4))
+    start_pair(join_copies(0))
     for k in range(chunks):
         recv[k, me] = d_ref[me * chunks + k]
+    hrecv[me] = dh[me]
 
     @pl.when(first)
     def _():
         below[...] = jnp.zeros_like(below)
+        zlo[...] = jnp.zeros_like(zlo)
         lo[...] = jnp.zeros_like(lo)
 
     @pl.when(last)
     def _():
         above[...] = jnp.zeros_like(above)
+        zhi[...] = jnp.zeros_like(zhi)
         hi[...] = jnp.zeros_like(hi)
+
+    column_load(d_ref, c_ref, elems, (1, 2, 3))
+    join_rows(c_ref, None, None, None, None, v0, (1, 2, 3))
+
+    def send_shared(k):
+        wait_got(shared_copies(k))
+        half = 4 * elems
+        row = lax.broadcasted_iota(jnp.int32, (8, modes), 0)
+        for s in range(span):
+            tjoin[k, s, 0:half] = tsend[k, s, 0:half] + zlo[k, s, half:ab]
+            tjoin[k, s, half:ab] = tsend[k, s, half:ab] + zhi[k, s, 0:half]
+            if k == chunks - 1:
+                ends = tsend[k, s, ab : ab + 8]
+                ends = ends + jnp.where(row == 0, zlo[k, s, ab + 1 : ab + 2], 0.0)
+                ends = ends + jnp.where(row == 1, zhi[k, s, ab : ab + 1], 0.0)
+                tjoin[k, s, ab : ab + 8] = ends
+            to_span(s, lambda n: outer_copy(k, s, n).start())
+        rows = slice(0, ab + 8 if k == chunks - 1 else ab)
+        trecv[k, me, rows] = tjoin[k, me, rows]
 
     for k in range(chunks):
         for d in range(1, span):
-            state_copy(k, d).wait_recv()
+            state_copy(k, peer(d), d - 1).wait_recv()
         start_pair(row_copies(k))
         if k == 0:
             for copy in tables:
                 copy.wait()
         to_planes([recv.at[k]], inv, fld, 0)
+        if k == 0:
+            for d in range(1, span):
+                halo_copy(peer(d), d - 1).wait_recv()
+            to_planes([hrecv], inv, halo, 0)
+        else:
+            send_shared(k - 1)
         wait_got(row_copies(k))
         to_planes([below.at[k], above.at[k]], inv, fld, sr)
         outer_rows(fld, tags(k), elems, first, last)
-        pointwise(fld, r_ref, h_ref, elems)
-        spectral(r_ref, h_ref, fwd, tsend.at[k], functools.partial(tend_start, k))
-        trecv[k, me] = tsend[k, me]
+        pointwise(fld, halo, edge, carry, r_ref, h_ref, elems, k, chunks)
+
+        def send_inner(s):
+            to_span(s, lambda n: inner_copy(k, s, n).start())
+
+        spectral(r_ref, h_ref, fwd, tsend.at[k], send_inner)
+        start_pair(shared_copies(k))
+        rows = slice(ab + 8, 20 * elems + 8)
+        trecv[k, me, rows] = tsend[k, me, rows]
+        if k == 0:
+            wait_got(join_copies(0))
+            join_rows(c_ref, lo.at[0], hi.at[0], None, None, v0, (0, 4))
+            wait_sent(join_copies(0))
+    send_shared(chunks - 1)
 
     for k in range(chunks):
         for d in range(1, span):
-            tend_copy(k, d).wait_recv()
-    column_load(d_ref, trecv, c_ref, elems, (0, 4))
-    start_pair(join_copies(0))
-    column_load(d_ref, trecv, c_ref, elems, (1, 2, 3))
+            inner_copy(k, peer(d), d - 1).wait_recv()
+            outer_copy(k, peer(d), d - 1).wait_recv()
+        add_tendency(v0, trecv, elems, k, chunks)
+    add_ends(v0, trecv, elems, chunks)
+
     ids = me * modes + lax.broadcasted_iota(jnp.int32, (1, modes), 1)
     wave = lax.shift_right_logical(ids, 1).astype(f32) / KMODES
     shift = 1.0 + STIFF * wave * wave
@@ -462,29 +553,26 @@
     sums = []
     prev = None
     for n, (v, w) in enumerate(((v0, w0), (v1, w1), (v2, w2))):
-        join = functools.partial(
-            join_rows, c_ref, lo.at[n], hi.at[n], prev, theta, v, first, last
-        )
-        square = join((1, 2, 3))
-        stretch(v, c_ref, (1, 2, 3))
-        wait_got(join_copies(n))
-        sums.append(square + join((0, 4)))
-        wait_sent(join_copies(n))
+        if n > 0:
+            join = functools.partial(join_rows, c_ref, lo.at[n], hi.at[n], prev, theta, v)
+            join((1, 2, 3))
+            stretch(v, c_ref, (1, 2, 3))
+            wait_got(join_copies(n))
+            join((0, 4))
+            wait_sent(join_copies(n))
         stretch(v, c_ref, (0, 4))
         outer = image(v, c_ref, shift, (0, 4))
         if n < 2:
             start_pair(join_copies(n + 1))
+        if n == 0:
+            stretch(v, c_ref, (1, 2, 3))
+        sums.append(squares(v, first, last, range(5)))
         sums.append(outer + image(v, c_ref, shift, (1, 2, 3)))
         if n < 2:
             unpack(v, expand, w)
         prev = v
     rows = [jnp.sum(t, axis=0, keepdims=True) for t in sums]
     part[...] = jnp.concatenate(rows + [jnp.zeros_like(rows[0])] * 2, axis=0)
-
-    def part_copy(d):
-        to = {"plane": lax.rem(mp + d, planes)}
-        return remote(part, parts.at[mp], s5.at[d - 1], r5.at[d - 1], to)
-
     for d in range(1, planes):
         part_copy(d).start()
     parts[mp] = part[...]
@@ -499,13 +587,28 @@
     y0, y1, y2 = y[:, 0:1], y[:, 1:2], y[:, 2:3]
     for j in range(5):
         out_ref[j] = y0 * w0[j] + y1 * w1[j] + y2 * w2[j]
+    for d in range(1, span):
+        halo_copy(peer(d), d - 1).wait_send()
     for k in range(chunks):
         for d in range(1, span):
-            state_copy(k, d).wait_send()
-            tend_copy(k, d).wait_send()
+            state_copy(k, peer(d), d - 1).wait_send()
+            inner_copy(k, peer(d), d - 1).wait_send()
+            outer_copy(k, peer(d), d - 1).wait_send()
         wait_sent(row_copies(k))
+        wait_sent(shared_copies(k))
     for d in range(1, planes):
         part_copy(d).wait_send()
+
+
+def place(x_hbm, out_hbm, sems):
+    copies = [
+        pltpu.make_async_copy(x_hbm.at[j], out_hbm.at[j], sems.at[j])
+        for j in range(x_hbm.shape[0])
+    ]
+    for copy in copies:
+        copy.start()
+    for copy in copies:
+        copy.wait()
 
 
 def shape(*dims):
@@ -521,7 +624,8 @@
     chunks = mine // 8
     elems = mine // chunks
     bl = 5 * elems
-    sr, tr = 5 * bl + PAD, 20 * elems + PAD
+    sr, tr, shared = 5 * bl, 20 * elems + 8, 8 * elems + 8
+    halos = -(-5 * (chunks + 1) // 8) * 8
     inverse, inner, outer = basis_tables()
     inv = jnp.asarray(np.stack(halves(inverse)))
     fwd = jnp.asarray(np.stack(halves(inner) + halves(outer)))
@@ -545,20 +649,31 @@
             pltpu.VMEM(expand.shape, bf16),
             buf(5, modes, cols), buf(5, modes, cols), buf(5, modes, cols),
             buf(span * chunks, sr, modes),
+            buf(span, halos, modes),
             buf(chunks, span, sr, modes),
+            buf(span, halos, modes),
             buf(chunks, span, bl, modes),
             buf(chunks, span, bl, modes),
             buf(sr + 2 * bl, PLANES),
+            buf(halos, PLANES),
+            buf(8, PLANES),
+            buf(16, PLANES),
             buf(tr, PLANES),
             buf(tr, PLANES),
             buf(chunks, span, tr, modes),
+            buf(chunks, span, shared, modes),
+            buf(chunks, span, shared, modes),
+            buf(chunks, span, shared, modes),
             buf(chunks, span, tr, modes),
             joined, joined, joined, joined, halo, halo,
             buf(8, modes),
             buf(planes, 8, modes),
             dma(3),
             dma(chunks, span - 1), dma(chunks, span - 1),
+            dma(span - 1), dma(span - 1),
             dma(chunks, 2), dma(chunks, 2),
+            dma(chunks, 2), dma(chunks, 2),
+            dma(chunks, span - 1), dma(chunks, span - 1),
             dma(chunks, span - 1), dma(chunks, span - 1),
             dma(3, 2), dma(3, 2),
             dma(planes - 1), dma(planes - 1),
@@ -567,6 +682,13 @@
             vmem_limit_bytes=VMEM_LIMIT, collective_id=0, has_side_effects=True
         ),
     )(state.transpose(1, 0, 2), perm, wall_tag.reshape(1, total), inv, fwd, expand)
+    out = pl.pallas_call(
+        place,
+        out_shape=shape(5, modes, cols),
+        in_specs=[hbm],
+        out_specs=hbm,
+        scratch_shapes=[dma(5)],
+    )(out)
     return out.transpose(1, 0, 2)
 
 

time: 70 us -> 122 us (1.74)
  Pallas kernels: 67.1 us -> 122 us
  local copies, waits for them, and re-layouts: 2.71 us -> 0 us
    pallas_call x0 -> x1, Pallas kernels: none -> 50.8 us  [on_device(): pl.pallas_call(place, out_shape=shape(5, modes, cols), in_specs=[hbm], ou...]
    pallas_call x1, Pallas kernels: 67.1 us -> 70.7 us  [on_device(): pl.pallas_call(functools.partial(segment, (span, planes, chunks, elems)),...]
    unnamed x1 -> x0, local copies, waits for them, and re-layouts: 2.71 us -> none
where the time goes in v3:
time: 122 us
  Pallas kernels  122 us (100%)
    pallas_call x1, Pallas kernels, on_device(): pl.pallas_call(functools.partial(segment, (span, planes, chunks, elems)),...  70.7 us
    pallas_call x1, Pallas kernels, on_device(): pl.pallas_call(place, out_shape=shape(5, modes, cols), in_specs=[hbm], ou...  50.8 us

profile of v3, /device:TPU:0, one launch (start us, length us, event | category | flops | bytes accessed | tf_op | source)
XLA Modules:
  0.0 121.7 jit_solution(7004006850290178928)
XLA Ops:
  0.0 70.7 %shard_map.64.x_hbm = f32[5,128,640]{2,1,0:T(8,128)} custom-call(f32[5,128,640]{2,1,0:T(8,128)} %bitcast.3, bf16[4,160,256]{2,1,0:T(8,128)(2,1)} %constant.10.clone.perm_ref, s32[1,128]{1,0:T(1,128)} %bitcast.4, bf16[2,512,768]{2,1,0:T(8,128)(2,1)} %constant.8.clone.inv_hbm, bf16[4,768,512]{2,1,0:T(8,128)(2,1)} %constant.9.clone.fwd_hbm, ...), custom_call_target="tpu_custom_call" | custom-call | tf_op jit(solution)/shard_map/pallas_call | solution.py:641
  70.7 50.8 %shard_map.65 = f32[5,128,640]{2,1,0:T(8,128)} custom-call(f32[5,128,640]{2,1,0:T(8,128)} %shard_map.64.x_hbm), custom_call_target="tpu_custom_call" | custom-call | tf_op jit(solution)/shard_map/pallas_call | solution.py:685

commit v4 on v3

--- a/solution.py
+++ b/solution.py
@@ -90,7 +90,7 @@
     return pltpu.roll(x, by % x.shape[0], 0)
 
 
-def pack(x_ref, perm_ref, d_ref, halo_ref, span, chunks, elems, ready):
+def pack(x_ref, perm_ref, d_ref, halo_ref, span, chunks, elems):
     rows, modes, cols = x_ref.shape
     block = 5 * elems
     wide = block * chunks
@@ -106,7 +106,6 @@
                 d_ref[s * chunks + k, block * j : block * (j + 1), :] = got[
                     block * k : block * (k + 1), modes * j : modes * (j + 1)
                 ]
-        ready(s)
     for s in range(span):
         left = (s * chunks - 1) % blocks
         for j in range(rows):
@@ -224,7 +223,7 @@
     lax.fori_loop(0, PLANES // lane, body, 0)
 
 
-def spectral(r_ref, h_ref, fwd_ref, t_ref, send):
+def spectral(r_ref, h_ref, fwd_ref, t_ref):
     span, _, modes = t_ref.shape
     rh, rl = split2(r_ref[...])
     hh, hl = split2(h_ref[...])
@@ -237,7 +236,6 @@
         for k in range(step // modes):
             s = n * (step // modes) + k
             t_ref[s] = t[:, modes * k : modes * (k + 1)]
-            send(s)
 
 
 def column_load(d_ref, c_ref, elems, js):
@@ -399,9 +397,10 @@
     for copy in tables:
         copy.start()
 
-    def to_span(s, start):
-        off = lax.rem(s - me + span, span)
-        pl.when(off > 0)(lambda: start(off - 1))
+    def to_peers(start):
+        for i in range(span - 1):
+            d = 1 + lax.rem(i + lax.rem(mp, 2) * (span // 2 - 1), span - 1)
+            start(peer(d), d - 1)
 
     def state_copy(k, s, n):
         src = d_ref.at[s * chunks + k]
@@ -459,19 +458,10 @@
         pl.when(inner)(pair[0].wait_recv)
         pl.when(beyond)(pair[1].wait_recv)
 
-    def ready(s):
-        if s == 0:
-            pl.semaphore_wait(barrier, span + planes - 2)
-        to_span(s, lambda n: state_copy(0, s, n).start())
-
-    pack(x_ref, perm_ref, d_ref, dh, span, chunks, elems, ready)
-    for s in range(span):
-        to_span(s, lambda n: halo_copy(s, n).start())
-    for k in range(1, chunks):
-        for s in range(span):
-            to_span(s, lambda n: state_copy(k, s, n).start())
-    column_load(d_ref, c_ref, elems, (0, 4))
-    start_pair(join_copies(0))
+    pack(x_ref, perm_ref, d_ref, dh, span, chunks, elems)
+    pl.semaphore_wait(barrier, span + planes - 2)
+    to_peers(lambda s, n: state_copy(0, s, n).start())
+    to_peers(lambda s, n: halo_copy(s, n).start())
     for k in range(chunks):
         recv[k, me] = d_ref[me * chunks + k]
     hrecv[me] = dh[me]
@@ -488,7 +478,7 @@
         zhi[...] = jnp.zeros_like(zhi)
         hi[...] = jnp.zeros_like(hi)
 
-    column_load(d_ref, c_ref, elems, (1, 2, 3))
+    column_load(d_ref, c_ref, elems, range(5))
     join_rows(c_ref, None, None, None, None, v0, (1, 2, 3))
 
     def send_shared(k):
@@ -503,7 +493,7 @@
                 ends = ends + jnp.where(row == 0, zlo[k, s, ab + 1 : ab + 2], 0.0)
                 ends = ends + jnp.where(row == 1, zhi[k, s, ab : ab + 1], 0.0)
                 tjoin[k, s, ab : ab + 8] = ends
-            to_span(s, lambda n: outer_copy(k, s, n).start())
+        to_peers(lambda s, n: outer_copy(k, s, n).start())
         rows = slice(0, ab + 8 if k == chunks - 1 else ab)
         trecv[k, me, rows] = tjoin[k, me, rows]
 
@@ -511,6 +501,10 @@
         for d in range(1, span):
             state_copy(k, peer(d), d - 1).wait_recv()
         start_pair(row_copies(k))
+        if k < chunks - 1:
+            to_peers(lambda s, n: state_copy(k + 1, s, n).start())
+        else:
+            start_pair(join_copies(0))
         if k == 0:
             for copy in tables:
                 copy.wait()
@@ -526,18 +520,15 @@
         outer_rows(fld, tags(k), elems, first, last)
         pointwise(fld, halo, edge, carry, r_ref, h_ref, elems, k, chunks)
 
-        def send_inner(s):
-            to_span(s, lambda n: inner_copy(k, s, n).start())
-
-        spectral(r_ref, h_ref, fwd, tsend.at[k], send_inner)
+        spectral(r_ref, h_ref, fwd, tsend.at[k])
         start_pair(shared_copies(k))
+        to_peers(lambda s, n: inner_copy(k, s, n).start())
         rows = slice(ab + 8, 20 * elems + 8)
         trecv[k, me, rows] = tsend[k, me, rows]
-        if k == 0:
-            wait_got(join_copies(0))
-            join_rows(c_ref, lo.at[0], hi.at[0], None, None, v0, (0, 4))
-            wait_sent(join_copies(0))
     send_shared(chunks - 1)
+    wait_got(join_copies(0))
+    join_rows(c_ref, lo.at[0], hi.at[0], None, None, v0, (0, 4))
+    wait_sent(join_copies(0))
 
     for k in range(chunks):
         for d in range(1, span):
@@ -600,15 +591,8 @@
         part_copy(d).wait_send()
 
 
-def place(x_hbm, out_hbm, sems):
-    copies = [
-        pltpu.make_async_copy(x_hbm.at[j], out_hbm.at[j], sems.at[j])
-        for j in range(x_hbm.shape[0])
-    ]
-    for copy in copies:
-        copy.start()
-    for copy in copies:
-        copy.wait()
+def place(x_ref, out_ref):
+    out_ref[...] = x_ref[...]
 
 
 def shape(*dims):
@@ -685,9 +669,9 @@
     out = pl.pallas_call(
         place,
         out_shape=shape(5, modes, cols),
-        in_specs=[hbm],
-        out_specs=hbm,
-        scratch_shapes=[dma(5)],
+        grid=(5,),
+        in_specs=[pl.BlockSpec((1, modes, cols), lambda j: (j, 0, 0))],
+        out_specs=pl.BlockSpec((1, modes, cols), lambda j: (j, 0, 0)),
     )(out)
     return out.transpose(1, 0, 2)
 

time: 122 us -> 71.5 us (0.59)
  Pallas kernels: 122 us -> 71.3 us
    pallas_call x1, Pallas kernels: 50.8 us -> 4.13 us  [on_device(): pl.pallas_call(place, out_shape=shape(5, modes, cols), grid=(5,), in_spec...]
    pallas_call x1, Pallas kernels: 70.7 us -> 67.2 us  [on_device(): pl.pallas_call(functools.partial(segment, (span, planes, chunks, elems)),...]
where the time goes in v4:
time: 71.5 us; the launch traced here: 71.3 us
  Pallas kernels  71.3 us (100%)
    pallas_call x1, Pallas kernels, on_device(): pl.pallas_call(functools.partial(segment, (span, planes, chunks, elems)),...  67.2 us
    pallas_call x1, Pallas kernels, on_device(): pl.pallas_call(place, out_shape=shape(5, modes, cols), grid=(5,), in_spec...  4.13 us

profile of v4, /device:TPU:0, one launch (start us, length us, event | category | flops | bytes accessed | tf_op | source)
XLA Modules:
  0.0 71.3 jit_solution(5023506426348807241)
XLA Ops:
  0.0 67.2 %shard_map.64.x_ref = f32[5,128,640]{2,1,0:T(8,128)} custom-call(f32[5,128,640]{2,1,0:T(8,128)} %bitcast.3, bf16[4,160,256]{2,1,0:T(8,128)(2,1)} %constant.10.clone.perm_ref, s32[1,128]{1,0:T(1,128)} %bitcast.4, bf16[2,512,768]{2,1,0:T(8,128)(2,1)} %constant.8.clone.inv_hbm, bf16[4,768,512]{2,1,0:T(8,128)(2,1)} %constant.9.clone.fwd_hbm, ...), custom_call_target="tpu_custom_call" | custom-call | tf_op jit(solution)/shard_map/pallas_call | solution.py:625
  67.2 4.1 %shard_map.65 = f32[5,128,640]{2,1,0:T(8,128)} custom-call(f32[5,128,640]{2,1,0:T(8,128)} %shard_map.64.x_ref), custom_call_target="tpu_custom_call" | custom-call | tf_op jit(solution)/shard_map/pallas_call | solution.py:669

commit v5 on v4

--- a/solution.py
+++ b/solution.py
@@ -60,8 +60,18 @@
     return high, (x - high.astype(f32)).astype(bf16)
 
 
+def stack2(x):
+    return jnp.concatenate([x, x - x.astype(bf16).astype(f32)], axis=0).astype(bf16)
+
+
 def dot(a, b, dims=NN):
     return lax.dot_general(a, b, dims, preferred_element_type=f32)
+
+
+def dot3(stacked, high, low):
+    rows = stacked.shape[0] // 2
+    both = dot(stacked, high)
+    return both[:rows] + both[rows:] + dot(stacked[:rows], low)
 
 
 def along(mat, a, flip):
@@ -137,11 +147,11 @@
     x = jnp.concatenate(
         [jnp.concatenate([p[s] for s in range(p.shape[0])], axis=1) for p in parts], axis=0
     )
-    high, low = split2(x)
+    stacked = stack2(x)
     for n in range(PLANES // 256):
         at = slice(n * 256, (n + 1) * 256)
         bh, bl = inv_ref[0, :, at], inv_ref[1, :, at]
-        fld_ref[lo : lo + x.shape[0], at] = dot(high, bh) + dot(high, bl) + dot(low, bh)
+        fld_ref[lo : lo + x.shape[0], at] = dot3(stacked, bh, bl)
 
 
 def outer_rows(fld_ref, tag, elems, first, last):
@@ -225,14 +235,13 @@
 
 def spectral(r_ref, h_ref, fwd_ref, t_ref):
     span, _, modes = t_ref.shape
-    rh, rl = split2(r_ref[...])
-    hh, hl = split2(h_ref[...])
+    rs, hs = stack2(r_ref[...]), stack2(h_ref[...])
     step = max(modes, 256)
     for n in range(span * modes // step):
         at = slice(n * step, (n + 1) * step)
         a, b = fwd_ref[0, :, at], fwd_ref[1, :, at]
         c, d = fwd_ref[2, :, at], fwd_ref[3, :, at]
-        t = dot(rh, a) + dot(rl, a) + dot(rh, b) + dot(hh, c) + dot(hl, c) + dot(hh, d)
+        t = dot3(rs, a, b) + dot3(hs, c, d)
         for k in range(step // modes):
             s = n * (step // modes) + k
             t_ref[s] = t[:, modes * k : modes * (k + 1)]
@@ -282,26 +291,40 @@
 COLW = [2.0 * WEIGHT[0], WEIGHT[1], WEIGHT[2], WEIGHT[3]]
 
 
-def stretch(v_ref, out_ref, js):
-    for j in js:
-        a = [v_ref[j, i] for i in range(4)]
-        a.append(roll(a[0], -1))
-        kx = along(KMAT * (VISCOUS * WEIGHT[j]), a, 1)
-        kx[0] = kx[0] + roll(kx[4], 1)
+def image(v_ref, out_ref, shift):
+    total, modes = v_ref.shape[2:]
+    row = lax.broadcasted_iota(jnp.int32, (8, modes), 0)
+
+    def along_row(j, at, after):
+        a = [v_ref[j, i, at, :] for i in range(4)]
+        a.append(jnp.where(row == 7, after, roll(a[0], -1)))
+        return a, along(KMAT * (VISCOUS * WEIGHT[j]), a, 1)
+
+    end = slice(total - 8, total)
+    ends = tuple(roll(along_row(j, end, v_ref[j, 0, 0:1, :])[1][4], 1) for j in range(5))
+
+    def body(g, carried):
+        before, acc = carried
+        at = pl.ds(pl.multiple_of(g * 8, 8), 8)
+        after = pl.ds(lax.rem(g * 8 + 8, total), 1)
+        vals, kx, tails = [], [], []
+        for j in range(5):
+            a, k = along_row(j, at, v_ref[j, 0, after, :])
+            tail = roll(k[4], 1)
+            k[0] = k[0] + jnp.where(row == 0, before[j], tail)
+            tails.append(tail)
+            vals.append(a)
+            kx.append(k)
         for i in range(4):
-            out_ref[j, i] = kx[i]
-
-
-def image(v_ref, out_ref, shift, js):
-    total = 0.0
-    for i in range(4):
-        a = [v_ref[j, i] for j in range(5)]
-        ky = along(KMAT * (VISCOUS * COLW[i]), a, 1)
-        for j in js:
-            val = out_ref[j, i] + ky[j] + (shift * float(WEIGHT[j] * COLW[i])) * a[j]
-            out_ref[j, i] = val
-            total = total + fold(val * a[j])
-    return total
+            col = [vals[j][i] for j in range(5)]
+            ky = along(KMAT * (VISCOUS * COLW[i]), col, 1)
+            for j in range(5):
+                val = kx[j][i] + ky[j] + (shift * float(WEIGHT[j] * COLW[i])) * col[j]
+                out_ref[j, i, at, :] = val
+                acc = acc + val * col[j]
+        return tuple(tails), acc
+
+    return lax.fori_loop(0, total // 8, body, (ends, jnp.zeros((8, modes), f32)))[1]
 
 
 def join_rows(c_ref, lo, hi, prev, theta, v_ref, js):
@@ -547,18 +570,14 @@
         if n > 0:
             join = functools.partial(join_rows, c_ref, lo.at[n], hi.at[n], prev, theta, v)
             join((1, 2, 3))
-            stretch(v, c_ref, (1, 2, 3))
             wait_got(join_copies(n))
             join((0, 4))
             wait_sent(join_copies(n))
-        stretch(v, c_ref, (0, 4))
-        outer = image(v, c_ref, shift, (0, 4))
+        curve = image(v, c_ref, shift)
         if n < 2:
             start_pair(join_copies(n + 1))
-        if n == 0:
-            stretch(v, c_ref, (1, 2, 3))
         sums.append(squares(v, first, last, range(5)))
-        sums.append(outer + image(v, c_ref, shift, (1, 2, 3)))
+        sums.append(curve)
         if n < 2:
             unpack(v, expand, w)
         prev = v
@@ -589,10 +608,6 @@
         wait_sent(shared_copies(k))
     for d in range(1, planes):
         part_copy(d).wait_send()
-
-
-def place(x_ref, out_ref):
-    out_ref[...] = x_ref[...]
 
 
 def shape(*dims):
@@ -666,13 +681,6 @@
             vmem_limit_bytes=VMEM_LIMIT, collective_id=0, has_side_effects=True
         ),
     )(state.transpose(1, 0, 2), perm, wall_tag.reshape(1, total), inv, fwd, expand)
-    out = pl.pallas_call(
-        place,
-        out_shape=shape(5, modes, cols),
-        grid=(5,),
-        in_specs=[pl.BlockSpec((1, modes, cols), lambda j: (j, 0, 0))],
-        out_specs=pl.BlockSpec((1, modes, cols), lambda j: (j, 0, 0)),
-    )(out)
     return out.transpose(1, 0, 2)
 
 

time: 71.5 us -> 71.3 us (level)
  Pallas kernels: 71.3 us -> 68.5 us
  local copies, waits for them, and re-layouts: 0 us -> 2.71 us
    pallas_call x1 -> x0, Pallas kernels: 4.13 us -> none  [on_device(): pl.pallas_call(place, out_shape=shape(5, modes, cols), grid=(5,), in_spec...]
    unnamed x0 -> x1, local copies, waits for them, and re-layouts: none -> 2.71 us
    pallas_call x1, Pallas kernels: 67.2 us -> 68.5 us  [on_device(): pl.pallas_call(functools.partial(segment, (span, planes, chunks, elems)),...]
where the time goes in v5:
time: 71.3 us; the launch traced here: 71.2 us
  Pallas kernels  68.5 us (96%)
  local copies, waits for them, and re-layouts  2.71 us (4%)
    pallas_call x1, Pallas kernels, on_device(): pl.pallas_call(functools.partial(segment, (span, planes, chunks, elems)),...  68.5 us
    unnamed x1, local copies, waits for them, and re-layouts  2.71 us

profile of v5, /device:TPU:0, one launch (start us, length us, event | category | flops | bytes accessed | tf_op | source)
XLA Modules:
  0.0 71.2 jit_solution(13774592454837675536)
XLA Ops:
  0.0 68.5 %shard_map.64 = f32[5,128,640]{2,1,0:T(8,128)} custom-call(f32[5,128,640]{2,1,0:T(8,128)} %bitcast.4, bf16[4,160,256]{2,1,0:T(8,128)(2,1)} %constant.10.clone.perm_ref, s32[1,128]{1,0:T(1,128)} %bitcast.5, bf16[2,512,768]{2,1,0:T(8,128)(2,1)} %constant.8.clone.inv_hbm, bf16[4,768,512]{2,1,0:T(8,128)(2,1)} %constant.9.clone.fwd_hbm, ...), custom_call_target="tpu_custom_call" | custom-call | tf_op jit(solution)/shard_map/pallas_call | solution.py:640
  68.5 2.7 %copy.8 = f32[128,5,640]{2,0,1:T(8,128)} copy(f32[128,5,640]{2,0,1:T(8,128)} %bitcast.3) | data formatting | bytes 3276800

commit v6 on v5

--- a/solution.py
+++ b/solution.py
@@ -172,7 +172,7 @@
     block = 5 * elems
     sr = 5 * block
     lane = 128
-    place = {0: 0, 4: 4 * elems}
+    place = {0: 0, 4: 4 * elems + 8}
     for j in (1, 2, 3):
         place[j] = 4 * elems * (j + 1) + 8
     third = DIFF * (-1.0 / 3.0)
@@ -221,13 +221,13 @@
                     ref[to : to + elems, at] = a[i]
                 tail = a[4][elems - 1 : elems, :]
                 if k == chunks - 1:
-                    ref[8 * elems + n : 8 * elems + n + 1, at] = tail
+                    ref[4 * elems + n : 4 * elems + n + 1, at] = tail
                 else:
                     carry_ref[base + j : base + j + 1, at] = tail
             if k == chunks - 1:
-                ref[8 * elems + 5 : 8 * elems + 8, at] = jnp.zeros((3, lane), f32)
+                ref[4 * elems + 5 : 4 * elems + 8, at] = jnp.zeros((3, lane), f32)
             else:
-                ref[8 * elems : 8 * elems + 8, at] = jnp.zeros((8, lane), f32)
+                ref[4 * elems : 4 * elems + 8, at] = jnp.zeros((8, lane), f32)
         return 0
 
     lax.fori_loop(0, PLANES // lane, body, 0)
@@ -267,7 +267,7 @@
 def add_tendency(v_ref, t_ref, elems, k, chunks):
     span = t_ref.shape[1]
     for j in range(5):
-        base = {0: 0, 4: 4 * elems}.get(j, 4 * elems * (j + 1) + 8)
+        base = {0: 0, 4: 4 * elems + 8}.get(j, 4 * elems * (j + 1) + 8)
         for s in range(span):
             at = slice(elems * (s * chunks + k), elems * (s * chunks + k + 1))
             for i in range(4):
@@ -279,7 +279,7 @@
     span = t_ref.shape[1]
     for n, j in enumerate((0, 4, 1, 2, 3)):
         for s in range(span):
-            end = t_ref[chunks - 1, (s - 1) % span, 8 * elems + n : 8 * elems + n + 1, :]
+            end = t_ref[chunks - 1, (s - 1) % span, 4 * elems + n : 4 * elems + n + 1, :]
             at = elems * s * chunks
             v_ref[j, 0, at : at + 1, :] += end * float(WEIGHT[j] * WEIGHT[0])
 
@@ -438,9 +438,9 @@
         return a, b
 
     def shared_copies(k):
-        src = tsend.at[k, :, 0 : ab + 8, :]
-        a = remote(src, zlo.at[k], sz.at[k, 0], rz.at[k, 0], up)
-        b = remote(src, zhi.at[k], sz.at[k, 1], rz.at[k, 1], down)
+        top, low = slice(4 * elems, ab + 8), slice(0, 4 * elems + 8)
+        a = remote(tsend.at[k, :, top, :], zlo.at[k], sz.at[k, 0], rz.at[k, 0], up)
+        b = remote(tsend.at[k, :, low, :], zhi.at[k], sz.at[k, 1], rz.at[k, 1], down)
         return a, b
 
     def inner_copy(k, s, n):
@@ -449,7 +449,7 @@
         return remote(src, dst, s3.at[k, n], r3.at[k, n], {"span": s})
 
     def outer_copy(k, s, n):
-        rows = slice(0, ab + 8 if k == chunks - 1 else ab)
+        rows = slice(0, ab + 8)
         src, dst = tjoin.at[k, s, rows, :], trecv.at[k, me, rows, :]
         return remote(src, dst, s6.at[k, n], r6.at[k, n], {"span": s})
 
@@ -509,15 +509,15 @@
         half = 4 * elems
         row = lax.broadcasted_iota(jnp.int32, (8, modes), 0)
         for s in range(span):
-            tjoin[k, s, 0:half] = tsend[k, s, 0:half] + zlo[k, s, half:ab]
-            tjoin[k, s, half:ab] = tsend[k, s, half:ab] + zhi[k, s, 0:half]
+            tjoin[k, s, 0:half] = tsend[k, s, 0:half] + zlo[k, s, 8 : half + 8]
+            tjoin[k, s, half + 8 :] = tsend[k, s, half + 8 : ab + 8] + zhi[k, s, 0:half]
+            ends = tsend[k, s, half : half + 8]
             if k == chunks - 1:
-                ends = tsend[k, s, ab : ab + 8]
-                ends = ends + jnp.where(row == 0, zlo[k, s, ab + 1 : ab + 2], 0.0)
-                ends = ends + jnp.where(row == 1, zhi[k, s, ab : ab + 1], 0.0)
-                tjoin[k, s, ab : ab + 8] = ends
+                ends = ends + jnp.where(row == 0, zlo[k, s, 1:2], 0.0)
+                ends = ends + jnp.where(row == 1, zhi[k, s, half : half + 1], 0.0)
+            tjoin[k, s, half : half + 8] = ends
         to_peers(lambda s, n: outer_copy(k, s, n).start())
-        rows = slice(0, ab + 8 if k == chunks - 1 else ab)
+        rows = slice(0, ab + 8)
         trecv[k, me, rows] = tjoin[k, me, rows]
 
     for k in range(chunks):
@@ -660,8 +660,8 @@
             buf(tr, PLANES),
             buf(tr, PLANES),
             buf(chunks, span, tr, modes),
-            buf(chunks, span, shared, modes),
-            buf(chunks, span, shared, modes),
+            buf(chunks, span, 4 * elems + 8, modes),
+            buf(chunks, span, 4 * elems + 8, modes),
             buf(chunks, span, shared, modes),
             buf(chunks, span, tr, modes),
             joined, joined, joined, joined, halo, halo,

time: 71.3 us -> 70.7 us (level)
  no operation moved by 1% of the time
where the time goes in v6:
time: 70.7 us; the launch traced here: 70.6 us
  Pallas kernels  67.9 us (96%)
  local copies, waits for them, and re-layouts  2.71 us (4%)
    pallas_call x1, Pallas kernels, on_device(): pl.pallas_call(functools.partial(segment, (span, planes, chunks, elems)),...  67.9 us
    unnamed x1, local copies, waits for them, and re-layouts  2.71 us

profile of v6, /device:TPU:0, one launch (start us, length us, event | category | flops | bytes accessed | tf_op | source)
XLA Modules:
  0.0 70.6 jit_solution(2820781936436476389)
XLA Ops:
  0.0 67.9 %shard_map.64 = f32[5,128,640]{2,1,0:T(8,128)} custom-call(f32[5,128,640]{2,1,0:T(8,128)} %bitcast.4, bf16[4,160,256]{2,1,0:T(8,128)(2,1)} %constant.10.clone.perm_ref, s32[1,128]{1,0:T(1,128)} %bitcast.5, bf16[2,512,768]{2,1,0:T(8,128)(2,1)} %constant.8.clone.inv_hbm, bf16[4,768,512]{2,1,0:T(8,128)(2,1)} %constant.9.clone.fwd_hbm, ...), custom_call_target="tpu_custom_call" | custom-call | tf_op jit(solution)/shard_map/pallas_call | solution.py:640
  67.9 2.7 %copy.8 = f32[128,5,640]{2,0,1:T(8,128)} copy(f32[128,5,640]{2,0,1:T(8,128)} %bitcast.3) | data formatting | bytes 3276800
